TPU v7x, 512 devices: a whole 4x4x16 slice. The times are simulated.
512 devices in a mesh: dp: 8 (over z_hi, y), shard: 64 (over x, z_lo, core).
Axes of the slice: x: 4, y: 4, z: 16 (z_hi: 2, z_lo: 8; z = z_hi * 8 + z_lo), core: 2. Of those that a mesh axis runs over, the one named last changes fastest.
Arguments:
- grad_out: bfloat16 [8, 16, 128, 8, 256], P('dp', None, 'shard'), may hold values from -6 to 6
- saved_mid: bfloat16 [8, 16, 64, 4, 512], P('dp', None, 'shard'), may hold values from -6 to 6
- norm_gain: float32 [512], replicated, may hold values from 0.25 to 1.75
- high_kernel: bfloat16 [512, 27, 256], P('shard'), may hold values from -0.078125 to 0.078125
- low_kernel: bfloat16 [256, 27, 512], P('shard'), may hold values from -0.0546875 to 0.0546875
Outputs:
- grad_in: bfloat16 [8, 64, 64, 1, 256], P('dp', 'shard')
- gain_grad: float32 [512], replicated
All inputs are finite; a program needn't handle non-finite values.
Results may differ from a plain program's by a relative error of at most 0.0049.
Values may be sent and summed in bfloat16 or wider, within the bound.
No kernel may reach another device: no remote copies, remote signals or barrier semaphores. Data moves between devices by JAX's collectives and lax.ppermute only.
A program may use at most 64 MiB of HBM per device.

v0:
```python
import math

import jax
import jax.numpy as jnp
from jax import lax
from jax.sharding import PartitionSpec as P

EPSILON = 1e-06
LAYOUT = ("NDHWC", "DHWIO", "NDHWC")


def padded(shard, sides, width):
    for axis, dim in sides:
        size, length = (lax.axis_size(axis), shard.shape[dim])
        up = [(i, (i + 1) % size) for i in range(size - 1)]
        down = [(j, i) for i, j in up]
        last = lax.slice_in_dim(shard, length - width, length, axis=dim)
        initial = lax.slice_in_dim(shard, 0, width, axis=dim)
        before = lax.ppermute(last, axis, up)
        after = lax.ppermute(initial, axis, down)
        shard = jnp.concatenate([before, shard, after], axis=dim)
    return shard


def shifted(shard, axis, by):
    size = lax.axis_size(axis)
    pairs = [(i, i + by) for i in range(size) if 0 <= i + by < size]
    return lax.ppermute(shard, axis, pairs)


def flipped(piece):
    count = piece.shape[0]
    outer = piece.shape[2]
    taps = piece.reshape(count, 3, 3, 3, outer)[:, ::-1, ::-1, ::-1, :]
    return jnp.transpose(taps, (1, 2, 3, 4, 0))


def transposed_conv(source, piece, margins):
    return lax.conv_general_dilated(
        source,
        flipped(piece),
        (1, 1, 1),
        margins,
        dimension_numbers=LAYOUT,
        preferred_element_type=jnp.float32,
    )


def place_channels(margins, source, total, piece, start):
    result = transposed_conv(source, piece, margins)
    return lax.dynamic_update_slice_in_dim(total, result, start, 4)


def shards(grad_out, saved_mid, norm_gain, high_kernel, low_kernel):
    high_margins = ((0, 2), (0, 0), (1, 1))
    low_margins = ((0, 0), (1, 1), (0, 0))
    clip_count = grad_out.shape[0]
    frames = grad_out.shape[1]
    rows_high = grad_out.shape[2]
    cols_high = grad_out.shape[3]
    rows_dev = saved_mid.shape[2]
    cols_low = saved_mid.shape[3]
    channels = saved_mid.shape[4]
    parts = lax.axis_size("shard")
    split = parts // frames
    col_dev = cols_low // split
    padded_grad = padded(grad_out, (("shard", 2),), 1)
    high_zero = jnp.zeros((clip_count, frames, rows_high, cols_high, channels), jnp.float32)
    norm_grad = place_channels(
        high_margins,
        padded_grad,
        high_zero,
        lax.all_gather(high_kernel, "shard", axis=0, tiled=True),
        jnp.int32(0),
    )
    blocks = norm_grad.reshape(clip_count, frames, rows_dev, 2, cols_low, 2, channels)
    mid_values = saved_mid.astype(jnp.float32)[:, :, :, None, :, None, :]
    inverse_rms = lax.rsqrt(jnp.mean(mid_values * mid_values, axis=-1, keepdims=True) + EPSILON)
    scaled = mid_values * inverse_rms
    normed = scaled * norm_gain
    gate_sig = jax.nn.sigmoid(normed)
    normed_grad = blocks * gate_sig * (1.0 + normed * (1.0 - gate_sig))
    local_gain = jnp.sum(normed_grad * scaled, axis=(0, 1, 2, 3, 4, 5))
    positions = lax.axis_size("dp") * clip_count * frames * rows_high * parts * cols_high
    gain_grad = lax.psum(local_gain, ("dp", "shard")) / math.sqrt(positions)
    gained = normed_grad * norm_gain
    pre_grad = inverse_rms * (gained - scaled * jnp.mean(gained * scaled, axis=-1, keepdims=True))
    mid_grad = jnp.sum(pre_grad, axis=(3, 5)).astype(jnp.bfloat16)
    sixfold = mid_grad.reshape(clip_count, frames, rows_dev, split, col_dev, channels)
    arranged = jnp.transpose(sixfold, (0, 1, 3, 2, 4, 5)).reshape(
        clip_count, parts, rows_dev, col_dev, channels
    )
    regrouped = lax.all_to_all(arranged, "shard", split_axis=1, concat_axis=2, tiled=True)
    following = shifted(regrouped, "shard", -split)
    further = shifted(regrouped, "shard", -2 * split)
    extended = jnp.concatenate([regrouped, following, further], axis=1)
    lower_rim = shifted(extended, "shard", 1)
    upper_rim = shifted(extended, "shard", -1)
    widened = jnp.concatenate([lower_rim, extended, upper_rim], axis=3)
    block = lax.axis_index("shard") % split
    column = lax.broadcasted_iota(jnp.int32, (col_dev + 2,), 0)
    keep = jnp.logical_and(
        jnp.logical_or(column > 0, block > 0),
        jnp.logical_or(column < col_dev + 1, block < split - 1),
    )
    widened = jnp.where(keep[:, None], widened, jnp.zeros_like(widened))
    inputs_low = low_kernel.shape[0] * parts
    low_zero = jnp.zeros((clip_count, 1, rows_dev * parts, col_dev, inputs_low), jnp.float32)
    low_result = place_channels(
        low_margins,
        widened,
        low_zero,
        lax.all_gather(low_kernel, "shard", axis=0, tiled=True),
        jnp.int32(0),
    )
    return (low_result.astype(jnp.bfloat16), gain_grad)


def solution(mesh):
    return jax.shard_map(
        shards,
        mesh=mesh,
        in_specs=(
            P("dp", None, "shard", None, None),
            P("dp", None, "shard", None, None),
            P(),
            P("shard", None, None),
            P("shard", None, None),
        ),
        out_specs=(P("dp", "shard", None, None, None), P()),
        check_vma=False,
    )
```

profile of v0, /device:TPU:2, one launch (start us, length us, event | category | flops | bytes accessed | tf_op | source)
XLA Modules:
  0.0 429.0 jit_solution(11670969244785099864)
XLA Ops:
  7.2 0.7 all-gather.3.cloned.1.call-update
  7.9 1.6 copy.58
  9.5 1.2 copy.52
  11.0 12.6 %collective-permute-start.1 = (bf16[1,16,1,8,256]{4,0,3,2,1:T(2,128)(2,1)S(1)}, bf16[1,16,1,8,256]{4,0,3,2,1:T(2,128)(2,1)S(1)}, u32[]{:S(2)}, u32[]{:S(2)}) collective-permute-start(bf16[1,16,1,8,256]{4,0,3,2,1:T(2,128)(2,1)S(1)} %get-tuple-element.17), channel_id=1, source_target_pairs={{1,0},{2,1},{3,2},{4,3},{5,4},{6,5},{7,6},{8,7},{9,8},{10,9},{11,1... | collective-permute-start | bytes 196616 | tf_op jit(solution)/shard_map/ppermute | solution.py:20
  23.6 1.9 collective-permute-start
  25.5 1.0 fusion.11
  26.5 1.0 add_divide_fusion
  28.6 8.9 %collective-permute-done = bf16[1,16,1,8,256]{4,0,3,2,1:T(2,128)(2,1)S(1)} collective-permute-done((bf16[1,16,1,8,256]{4,0,3,2,1:T(2,128)(2,1)S(1)}, bf16[1,16,1,8,256]{4,0,3,2,1:T(2,128)(2,1)S(1)}, u32[]{:S(2)}, u32[]{:S(2)}) %collective-permute-start) | collective-permute-done | bytes 65568 | tf_op jit(solution)/shard_map/ppermute | solution.py:19
  37.6 110.9 %all-gather.3.cloned.1.call-done = bf16[512,27,256]{2,0,1:T(8,128)(2,1)} async-done(((bf16[8,27,256]{2,0,1:T(8,128)(2,1)}), bf16[512,27,256]{2,0,1:T(8,128)(2,1)}) %all-gather.3.cloned.1.call-update) | async-done | bytes 7077904 | tf_op jit(solution)/shard_map/all_gather | solution.py:73
  148.5 15.6 %multiply_reduce_fusion.2 = (f32[16,2,8]{2,1,0:T(2,128)S(1)}, f32[1,16,2,8,512]{4,0,3,2,1:T(1,128)S(1)}) fusion(f32[16,8,512]{2,1,0:T(8,128)S(1)} %mul.179, f32[512]{0:T(512)} %param.7, f32[16,8,512]{2,1,0:T(8,128)S(1)} %mul.173, f32[16,8,512]{2,1,0:T(8,128)S(1)} %mul.168, bf16[512,3,3,3,256]{4,0,3,2,1:T(8,128)(2,1)} %bitcast.30, ...), kind=kOutput, calls=%fused_computation.13 | convolution fusion | flops 1558576896 | bytes 8653824 | tf_op jit(solution)/shard_map/conv_general_dilated | solution.py:39
  164.1 1.8 multiply_reduce_fusion
  166.7 1.0 reduce.9
  168.4 9.8 %all-to-all-start = ((bf16[64,2,256]{2,1,0:T(2,128)(2,1)}), bf16[64,2,256]{2,1,0:T(2,128)(2,1)S(1)}, u32[]{:S(2)}, u32[]{:S(2)}) async-start(bf16[64,2,256]{2,1,0:T(2,128)(2,1)} %reshape.170), calls=%async_computation | async-start | bytes 131072 | tf_op jit(solution)/shard_map/all_to_all | solution.py:93
  178.2 12.8 %all-to-all-done = bf16[64,2,256]{2,1,0:T(2,128)(2,1)S(1)} async-done(((bf16[64,2,256]{2,1,0:T(2,128)(2,1)}), bf16[64,2,256]{2,1,0:T(2,128)(2,1)S(1)}, u32[]{:S(2)}, u32[]{:S(2)}) %all-to-all-start) | async-done | bytes 65568 | tf_op jit(solution)/shard_map/all_to_all | solution.py:93
  191.1 2.1 collective-permute-start.3
  193.2 8.3 %collective-permute-start.2 = (bf16[1,1,64,1,512]{4,2,3,1,0:T(8,128)(2,1)S(1)}, bf16[1,1,64,1,512]{4,2,3,1,0:T(8,128)(2,1)S(1)}, u32[]{:S(2)}, u32[]{:S(2)}) collective-permute-start(bf16[1,1,64,1,512]{4,2,3,1,0:T(8,128)(2,1)S(1)} %bitcast.24), channel_id=1, source_target_pairs={{4,0},{5,1},{6,2},{7,3},{8,4},{9,5},{10,6},{11,7},{12,8},{13,9},{1... | collective-permute-start | bytes 196616 | tf_op jit(solution)/shard_map/ppermute | solution.py:28
  201.5 77.1 %all-gather.5.cloned.1.call-done = bf16[256,27,512]{2,1,0:T(8,128)(2,1)} async-done(((bf16[4,27,512]{2,1,0:T(8,128)(2,1)}), bf16[256,27,512]{2,1,0:T(8,128)(2,1)}) %all-gather.5.cloned.1.call-update) | async-done | bytes 7077904 | tf_op jit(solution)/shard_map/all_gather | solution.py:113
  278.7 10.4 %copy.59 = bf16[256,27,512]{2,0,1:T(8,128)(2,1)} copy(bf16[256,27,512]{2,1,0:T(8,128)(2,1)} %all-gather.5.cloned.1.call-done) | data formatting | bytes 14155776 | tf_op jit(solution)/shard_map/all_gather | solution.py:113
  289.1 105.0 %psum.7 = f32[512]{0:T(512)S(1)} all-reduce(f32[512]{0:T(512)S(1)} %get-tuple-element.14), channel_id=1, replica_groups=mesh['dp'=8,'shard'=64] {'dp','shard'}, use_global_device_ids=true, to_apply=%region_5.6 | all-reduce | flops 512 | bytes 4096 | tf_op jit(solution)/shard_map/psum | solution.py:85
  394.1 5.9 %collective-permute-start.5 = (bf16[1,3,64,1,512]{4,2,3,1,0:T(8,128)(2,1)S(1)}, bf16[1,3,64,1,512]{4,2,3,1,0:T(8,128)(2,1)S(1)}, u32[]{:S(2)}, u32[]{:S(2)}) collective-permute-start(bf16[1,3,64,1,512]{4,2,3,1,0:T(8,128)(2,1)S(1)} %pad_maximum_fusion), channel_id=1, source_target_pairs={{1,0},{2,1},{3,2},{4,3},{5,4},{6,5},{7,6},{8,7},{9,8},{10,9},{11,1... | collective-permute-start | bytes 589832 | tf_op jit(solution)/shard_map/ppermute | solution.py:28
  400.0 1.9 collective-permute-start.4
  402.5 1.6 collective-permute-done.5
  404.1 10.4 %collective-permute-done.4 = bf16[1,3,64,1,512]{4,2,3,1,0:T(8,128)(2,1)S(1)} collective-permute-done((bf16[1,3,64,1,512]{4,2,3,1,0:T(8,128)(2,1)S(1)}, bf16[1,3,64,1,512]{4,2,3,1,0:T(8,128)(2,1)S(1)}, u32[]{:S(2)}, u32[]{:S(2)}) %collective-permute-start.4) | collective-permute-done | bytes 196640 | tf_op jit(solution)/shard_map/ppermute | solution.py:28
  414.7 6.9 %fusion.3 = bf16[1,1,64,1,256]{4,0,3,2,1:T(2,128)(2,1)S(1)} fusion(bf16[256,3,3,3,512]{4,0,3,2,1:T(8,128)(2,1)} %bitcast.22, bf16[1,3,64,3,512]{4,2,3,1,0:T(8,128)(2,1)S(1)} %maximum_select_fusion), kind=kOutput, calls=%fused_computation.4 | convolution fusion | flops 448282624 | bytes 7700480 | tf_op jit(solution)/shard_map/conv_general_dilated | solution.py:39
  (32 shorter events, 4.3 us)
Async XLA Ops:
  7.2 141.3 %all-gather.3.cloned.1.call-start = ((), (), s32[]{:S(2)}) async-start(), calls=%async_computation.1 | async-start | bytes 7188480 | tf_op jit(solution)/shard_map/all_gather | solution.py:73
  7.9 270.8 %all-gather.5.cloned.1.call-start = ((), (), s32[]{:S(2)}) async-start(), calls=%async_computation.2 | async-start | bytes 8519680 | tf_op jit(solution)/shard_map/all_gather | solution.py:113
  11.0 17.6 %collective-permute-start.1 = (bf16[1,16,1,8,256]{4,0,3,2,1:T(2,128)(2,1)S(1)}, bf16[1,16,1,8,256]{4,0,3,2,1:T(2,128)(2,1)S(1)}, u32[]{:S(2)}, u32[]{:S(2)}) collective-permute-start(bf16[1,16,1,8,256]{4,0,3,2,1:T(2,128)(2,1)S(1)} %get-tuple-element.17), channel_id=1, source_target_pairs={{1,0},{2,1},{3,2},{4,3},{5,4},{6,5},{7,6},{8,7},{9,8},{10,9},{11,1... | collective-permute-start | bytes 196616 | tf_op jit(solution)/shard_map/ppermute | solution.py:20
  23.6 14.0 %collective-permute-start = (bf16[1,16,1,8,256]{4,0,3,2,1:T(2,128)(2,1)S(1)}, bf16[1,16,1,8,256]{4,0,3,2,1:T(2,128)(2,1)S(1)}, u32[]{:S(2)}, u32[]{:S(2)}) collective-permute-start(bf16[1,16,1,8,256]{4,0,3,2,1:T(2,128)(2,1)S(1)} %get-tuple-element.16), channel_id=1, source_target_pairs={{0,1},{1,2},{2,3},{3,4},{4,5},{5,6},{6,7},{7,8},{8,9},{9,10},{10,1... | collective-permute-start | bytes 196616 | tf_op jit(solution)/shard_map/ppermute | solution.py:19
  148.5 15.6 %copy-start = (f32[512]{0:T(512)S(1)}, f32[512]{0:T(512)}, u32[]{:S(2)}) copy-start(f32[512]{0:T(512)} %param.7) | copy-start | bytes 6148
  168.4 22.6 %all-to-all-start = ((bf16[64,2,256]{2,1,0:T(2,128)(2,1)}), bf16[64,2,256]{2,1,0:T(2,128)(2,1)S(1)}, u32[]{:S(2)}, u32[]{:S(2)}) async-start(bf16[64,2,256]{2,1,0:T(2,128)(2,1)} %reshape.170), calls=%async_computation | async-start | bytes 131072 | tf_op jit(solution)/shard_map/all_to_all | solution.py:93
  191.1 203.0 %collective-permute-start.3 = (bf16[1,1,64,1,512]{4,2,3,1,0:T(8,128)(2,1)S(1)}, bf16[1,1,64,1,512]{4,2,3,1,0:T(8,128)(2,1)S(1)}, u32[]{:S(2)}, u32[]{:S(2)}) collective-permute-start(bf16[1,1,64,1,512]{4,2,3,1,0:T(8,128)(2,1)S(1)} %bitcast.23), channel_id=1, source_target_pairs={{8,0},{9,1},{10,2},{11,3},{12,4},{13,5},{14,6},{15,7},{16,8},{17,9... | collective-permute-start | bytes 196616 | tf_op jit(solution)/shard_map/ppermute | solution.py:28
  193.2 200.9 %collective-permute-start.2 = (bf16[1,1,64,1,512]{4,2,3,1,0:T(8,128)(2,1)S(1)}, bf16[1,1,64,1,512]{4,2,3,1,0:T(8,128)(2,1)S(1)}, u32[]{:S(2)}, u32[]{:S(2)}) collective-permute-start(bf16[1,1,64,1,512]{4,2,3,1,0:T(8,128)(2,1)S(1)} %bitcast.24), channel_id=1, source_target_pairs={{4,0},{5,1},{6,2},{7,3},{8,4},{9,5},{10,6},{11,7},{12,8},{13,9},{1... | collective-permute-start | bytes 196616 | tf_op jit(solution)/shard_map/ppermute | solution.py:28
  394.1 10.0 %collective-permute-start.5 = (bf16[1,3,64,1,512]{4,2,3,1,0:T(8,128)(2,1)S(1)}, bf16[1,3,64,1,512]{4,2,3,1,0:T(8,128)(2,1)S(1)}, u32[]{:S(2)}, u32[]{:S(2)}) collective-permute-start(bf16[1,3,64,1,512]{4,2,3,1,0:T(8,128)(2,1)S(1)} %pad_maximum_fusion), channel_id=1, source_target_pairs={{1,0},{2,1},{3,2},{4,3},{5,4},{6,5},{7,6},{8,7},{9,8},{10,9},{11,1... | collective-permute-start | bytes 589832 | tf_op jit(solution)/shard_map/ppermute | solution.py:28
  400.0 14.5 %collective-permute-start.4 = (bf16[1,3,64,1,512]{4,2,3,1,0:T(8,128)(2,1)S(1)}, bf16[1,3,64,1,512]{4,2,3,1,0:T(8,128)(2,1)S(1)}, u32[]{:S(2)}, u32[]{:S(2)}) collective-permute-start(bf16[1,3,64,1,512]{4,2,3,1,0:T(8,128)(2,1)S(1)} %pad_maximum_fusion), channel_id=1, source_target_pairs={{0,1},{1,2},{2,3},{3,4},{4,5},{5,6},{6,7},{7,8},{8,9},{9,10},{10,1... | collective-permute-start | bytes 589832 | tf_op jit(solution)/shard_map/ppermute | solution.py:28
Sparse Core Ops, SparseCore 0:
  10.1 138.3 all-gather.2
  150.6 127.9 all-gather.4
where the time goes:
time: 430 us; the launch traced here: 429 us
  waiting for transfers between devices  222 us (52%)
  blocking collectives  105 us (24%)
  starting transfers between devices  42.6 us (10%)
  matrix products  22.4 us (5%)
  local copies, waits for them, and re-layouts  16.5 us (4%)
  between operations  14.3 us (3%)
  other arithmetic  5.74 us (1%)
    all_gather x1, waiting for transfers between devices, shards(): lax.all_gather(high_kernel, 'shard', axis=0, tiled=True)  111 us
    psum x1, blocking collectives, shards(): gain_grad = lax.psum(local_gain, ('dp', 'shard')) / math.sqrt(positions)  105 us
    all_gather x1, waiting for transfers between devices, shards(): lax.all_gather(low_kernel, 'shard', axis=0, tiled=True)  77.1 us
    conv_general_dilated x2, matrix products, transposed_conv(): lax.conv_general_dilated(source, flipped(piece), (1, 1, 1), margins, dime...  22.4 us
    ppermute x4, starting transfers between devices, shifted(): return lax.ppermute(shard, axis, pairs)  18.2 us
    all_to_all x1, waiting for transfers between devices, shards(): lax.all_to_all(arranged, 'shard', split_axis=1, concat_axis=2, tiled=True)  12.8 us
    ppermute x1, starting transfers between devices, padded(): after = lax.ppermute(initial, axis, down)  12.6 us
    ppermute x4, waiting for transfers between devices, shifted(): return lax.ppermute(shard, axis, pairs)  12 us
  transfers between devices with their start and end apart: 9, of which 6 were waited for; matrix products, arithmetic and copies ran while one was open for 9% of the time, Pallas kernels for 0%

commit v1 on v0

v1 whole, which is shorter than its diff:
```python
import math

import jax
import jax.numpy as jnp
from jax import lax
from jax.experimental import pallas as pl
from jax.experimental.pallas import tpu as pltpu
from jax.sharding import Mesh
from jax.sharding import PartitionSpec as P

EPSILON = 1e-06
F32 = jnp.float32
BF16 = jnp.bfloat16
NEAR = (0, 1, -1, 2)
FAR = (4, -3, 3, -2)
OFFSETS = tuple(o for pair in zip(NEAR, FAR) for o in pair)
NT = (((1,), (1,)), ((), ()))


def iota(shape, dim):
    return lax.broadcasted_iota(jnp.int32, shape, dim)


def owner_z(slot, z):
    offset = jnp.zeros_like(slot)
    for n, o in enumerate(OFFSETS):
        offset = jnp.where(slot == n, o % 8, offset)
    return (z + offset) & 7


def row_shift(value, by):
    rows = value.shape[0]
    by = by % rows
    return value if by == 0 else pltpu.roll(value, rows - by, 0)


def half_turn(value):
    return pltpu.roll(value, 64, 1)


def full_mid(parts_ref, source):
    return jnp.concatenate(
        [parts_ref[source, 384:448, :], parts_ref[source, 448:512, :]], axis=1
    )


def inverse_rms(mid):
    return lax.rsqrt(jnp.mean(mid * mid, axis=1, keepdims=True) + EPSILON)


def high_kernel_body(place_ref, parts_ref, weight_ref, gain_ref, out_ref, gain_out_ref, taps_ref, wide_ref):
    x, c, z = place_ref[0], place_ref[1], place_ref[2]
    for dy in range(3):
        for dw in range(3):
            for dt in range(3):
                tap = 9 * (2 - dt) + 3 * (2 - dy) + dw
                for j in range(4):
                    at = (dw * 4 + dt) * 64 + 16 * j
                    taps_ref[dy, at : at + 16, :] = weight_ref[j, tap]
            at = (dw * 4 + 3) * 64
            taps_ref[dy, at : at + 64, :] = jnp.zeros((64, 256), BF16)
    row = iota((256, 256), 0)
    column_high = row & 7
    frame = (iota((256, 128), 0) >> 3) & 15
    low_half = iota((128, 128), 1) < 64
    for pair in range(4):
        rows = jnp.concatenate(
            [parts_ref[2 * pair, 0:384, :], parts_ref[2 * pair + 1, 0:384, :]], axis=0
        )
        product = sum(
            lax.dot_general(
                rows[128 * dy : 128 * dy + 512], taps_ref[dy], NT, preferred_element_type=F32
            )
            for dy in range(3)
        )
        pooled = jnp.concatenate(
            [product[0:128] + product[128:256], product[256:384] + product[384:512]], axis=0
        )
        after = jnp.where(column_high < 7, row_shift(pooled[:, 0:256], 1), 0.0)
        before = jnp.where(column_high > 0, row_shift(pooled[:, 512:768], -1), 0.0)
        moved = after + pooled[:, 256:512] + before
        moved = moved + row_shift(moved, 1)
        now, later = moved[:, 0:128], moved[:, 128:256]
        total = now
        total = total + jnp.where(frame < 15, row_shift(half_turn(now), 8), 0.0)
        total = total + jnp.where(frame < 14, row_shift(later, 16), 0.0)
        wide_ref[128 * pair : 128 * pair + 128, :] = jnp.where(
            low_half, total[0:128], half_turn(total[128:256])
        )
    summed = jnp.concatenate(
        [wide_ref[pl.ds(128 * pair, 64, stride=2), :] for pair in range(4)], axis=0
    )
    lane = iota((1, 128), 1)
    slot = (lane >> 3) & 7
    target = 128 * x + 16 * owner_z(slot, z) + 8 * c + (lane & 7)
    channel = iota((512, 128), 0)
    hit = channel == target
    half = iota((512, 128), 1) >> 6
    picks = [jnp.where(hit & (half == y), 1.0, 0.0).astype(BF16) for y in range(2)]
    mids = [
        jnp.concatenate([full_mid(parts_ref, 2 * pair + y) for pair in range(4)], axis=0)
        for y in range(2)
    ]
    mid = sum(
        jnp.dot(m, s, preferred_element_type=F32) for m, s in zip(mids, picks)
    )
    rms = [inverse_rms(m.astype(F32)) for m in mids]
    scaled = mid * jnp.where(iota((256, 128), 1) < 64, rms[0], rms[1])
    gain = jnp.dot(
        jnp.broadcast_to(gain_ref[...], (8, 512)),
        jnp.where(hit, 1.0, 0.0),
        precision=lax.Precision.HIGHEST,
        preferred_element_type=F32,
    )[0:1]
    normed = scaled * gain
    gate = jax.nn.sigmoid(normed)
    grad = summed * (gate * (1.0 + normed * (1.0 - gate)))
    out_ref[...] = (grad * gain).astype(BF16)
    terms = jnp.sum(grad * scaled, axis=0, keepdims=True)
    terms = terms + half_turn(terms)
    source = iota((128, 128), 0)
    place = (source & 64) + 8 * owner_z((source >> 3) & 7, z) + (source & 7)
    order = jnp.where(place == iota((128, 128), 1), 1.0, 0.0)
    gain_out_ref[...] = jnp.dot(
        jnp.broadcast_to(terms, (8, 128)),
        order,
        precision=lax.Precision.HIGHEST,
        preferred_element_type=F32,
    )


def low_kernel_body(place_ref, grads_ref, parts_ref, weight_ref, out_ref, turned_ref):
    z = place_ref[2]
    source = iota((256, 256), 0)
    target = (
        ((source >> 6) & 1) * 128
        + owner_z((source >> 3) & 7, z) * 16
        + (source >> 7) * 8
        + (source & 7)
    )
    order = jnp.where(target == iota((256, 256), 1), 1.0, 0.0).astype(BF16)
    placed = [
        jnp.dot(
            jnp.concatenate([grads_ref[2 * x], grads_ref[2 * x + 1]], axis=1),
            order,
            preferred_element_type=F32,
        )
        for x in range(4)
    ]
    halves = []
    for y in range(2):
        grad = jnp.concatenate([p[:, 128 * y : 128 * y + 128] for p in placed], axis=1)
        mid = jnp.concatenate(
            [full_mid(parts_ref, 2 * pair + y) for pair in range(4)], axis=0
        ).astype(F32)
        rms = inverse_rms(mid)
        scaled = mid * rms
        mean = jnp.mean(grad * scaled, axis=1, keepdims=True)
        halves.append((rms * (grad - scaled * mean)).astype(BF16))
    grads = jnp.concatenate(halves, axis=0)
    row = iota((512, 128), 0)
    frame = (row >> 2) & 15
    column = row & 3
    total = jnp.zeros((512, 128), F32)
    for a in range(3):
        for c in range(3):
            at = 16 * (3 * a + c)
            taps = jnp.concatenate([weight_ref[n, at : at + 16, :] for n in range(8)], axis=0)
            product = lax.dot_general(grads, taps, NT, preferred_element_type=F32)
            moved = row_shift(product, 4 * (2 - a) + 1 - c)
            keep = (frame + 2 - a < 16) & (column + 1 - c >= 0) & (column + 1 - c < 4)
            total = total + jnp.where(keep, moved, 0.0)
    result = total[0:256] + pltpu.roll(total[256:512], 4, 1)
    for pair in range(4):
        turned_ref[:, pair, :] = result[64 * pair : 64 * pair + 64]
    turned_ref[:, 4:8, :] = jnp.zeros((64, 4, 128), F32)
    out_ref[...] = turned_ref[...].astype(BF16)


def join_body(scale, parts_ref, out_ref, gain_ref):
    parts = parts_ref[...].astype(F32)
    strips = [
        jnp.concatenate([parts[16 * x + 2 * z + c] for z in range(8)], axis=0)
        for x in range(4)
        for c in range(2)
    ]
    wide = jnp.concatenate([s.astype(BF16) for s in strips], axis=1)
    lane = iota((64, 1024), 1)
    row_out = iota((64, 64), 0)
    row_in = iota((64, 64), 1)
    pair, z = row_in & 7, row_in >> 3
    joined = jnp.zeros((64, 1024), F32)
    for n in range(4):
        pick = (row_out == 16 * pair + 2 * z - 1 + n) & (pair < 4)
        placed = jnp.dot(
            jnp.where(pick, 1.0, 0.0).astype(BF16), wide, preferred_element_type=F32
        )
        joined = jnp.where(((lane >> 2) & 3) == n, placed, joined)
    source = iota((1024, 256), 0)
    target = (
        (source >> 8) * 64 + ((source >> 4) & 7) * 8 + ((source >> 7) & 1) * 4 + (source & 3)
    )
    order = jnp.where(target == iota((1024, 256), 1), 1.0, 0.0).astype(BF16)
    out_ref[...] = jnp.dot(
        joined.astype(BF16), order, preferred_element_type=F32
    ).astype(BF16)
    low_half = iota((1, 128), 1) < 64
    lines = []
    for x in range(4):
        pieces = []
        for c in range(2):
            piece = sum(parts[16 * x + 2 * z + c, 4:5, :] for z in range(8))
            pieces.append(piece + half_turn(piece))
        lines.append(jnp.where(low_half, pieces[0], pieces[1]))
    lines = jnp.concatenate(lines + lines, axis=0)
    source = iota((128, 128), 0)
    target = ((source >> 3) & 7) * 16 + (source >> 6) * 8 + (source & 7)
    order = jnp.where(target == iota((128, 128), 1), 1.0, 0.0)
    gain_ref[...] = (
        jnp.dot(lines, order, precision=lax.Precision.HIGHEST, preferred_element_type=F32)[0:4]
        * scale
    )


def whole():
    return pl.BlockSpec(memory_space=pltpu.VMEM)


def scalars():
    return pl.BlockSpec(memory_space=pltpu.SMEM)


PARAMS = pltpu.CompilerParams(vmem_limit_bytes=40 * 1024 * 1024)


def ring_pairs(distances):
    pairs = []
    for zh in range(2):
        for y in range(4):
            for zl in range(8):
                for c in range(2):
                    by = distances[y]
                    if by == 4 and c == 1:
                        by = -4
                    at = (zh * 8 + zl + by) % 16
                    source = ((at // 8 * 4 + y) * 8 + at % 8) * 2 + c
                    pairs.append((source, ((zh * 4 + y) * 8 + zl) * 2 + c))
    return pairs


def shards(grad_out, saved_mid, norm_gain, high_kernel, low_kernel):
    x, z, c = (lax.axis_index(n) for n in ("x", "zl", "c"))
    place = jnp.stack([x, c, z]).astype(jnp.int32)
    ring = ("zh", "y", "zl", "c")
    group = ("x", "c")
    shard = ("x", "zl", "c")

    low = jnp.transpose(low_kernel.reshape(4, 3, 3, 3, 512), (1, 3, 2, 0, 4))
    low = jnp.pad(low, ((0, 0), (0, 0), (0, 1), (0, 0), (0, 0))).reshape(144, 512)
    low_all = lax.all_gather(low, "zl", axis=0)

    grad = grad_out[0]
    edge = jnp.where(c == 0, grad[:, 0], grad[:, 1])
    halo_pairs = [(s, s - 1) for s in range(2, 64, 2)] + [(s, s + 1) for s in range(1, 62, 2)]
    halo = lax.ppermute(edge, shard, halo_pairs)

    high = jnp.transpose(high_kernel, (1, 0, 2))
    near = lax.ppermute(high, ring, ring_pairs(NEAR))
    far = lax.ppermute(high, ring, ring_pairs(FAR))

    own = jnp.transpose(grad, (1, 0, 2, 3)).reshape(256, 256)
    halo = halo.reshape(128, 256)
    rows = jnp.where(
        c == 0,
        jnp.concatenate([halo, own], axis=0),
        jnp.concatenate([own, halo], axis=0),
    )
    mid = saved_mid.reshape(64, 512)
    chunk = jnp.concatenate([rows, mid[:, 0:256], mid[:, 256:512]], axis=0)
    parts = lax.all_to_all(
        jnp.broadcast_to(chunk[None], (8, 512, 256)), group, split_axis=0, concat_axis=0, tiled=True
    )
    high_all = lax.all_gather(jnp.concatenate([near, far], axis=1), "y", axis=0)

    grads, gain_terms = pl.pallas_call(
        high_kernel_body,
        out_shape=(
            jax.ShapeDtypeStruct((256, 128), BF16),
            jax.ShapeDtypeStruct((8, 128), F32),
        ),
        in_specs=[scalars(), whole(), whole(), whole()],
        out_specs=(whole(), whole()),
        scratch_shapes=[pltpu.VMEM((3, 768, 256), BF16), pltpu.VMEM((512, 128), F32)],
        compiler_params=PARAMS,
        name="high_conv",
    )(place, parts, high_all, norm_gain.reshape(1, 512))

    gathered = lax.all_gather(grads, group, axis=0)
    for axis, pairs in (
        ("y", [(i, i ^ 1) for i in range(4)]),
        ("y", [(i, i ^ 2) for i in range(4)]),
        ("zh", [(0, 1), (1, 0)]),
    ):
        gain_terms = gain_terms + lax.ppermute(gain_terms, axis, pairs)

    partial = pl.pallas_call(
        low_kernel_body,
        out_shape=jax.ShapeDtypeStruct((64, 8, 128), BF16),
        in_specs=[scalars(), whole(), whole(), whole()],
        out_specs=whole(),
        scratch_shapes=[pltpu.VMEM((64, 8, 128), F32)],
        compiler_params=PARAMS,
        name="low_conv",
    )(place, gathered, parts, low_all)

    head = lax.reduce_precision(gain_terms, 8, 7)
    tail = gain_terms - head
    line = jnp.where(lax.broadcasted_iota(jnp.int32, (8, 128), 1) < 64, head, tail).astype(BF16)
    is_gain = lax.broadcasted_iota(jnp.int32, (64, 8, 128), 1) == 4
    outgoing = jnp.where(is_gain, line[None], partial)
    incoming = lax.all_to_all(outgoing, shard, split_axis=0, concat_axis=0, tiled=True)

    positions = 8 * 16 * 128 * 8
    grad_in, gain_grad = pl.pallas_call(
        lambda *refs: join_body(1.0 / math.sqrt(positions), *refs),
        out_shape=(
            jax.ShapeDtypeStruct((64, 256), BF16),
            jax.ShapeDtypeStruct((4, 128), F32),
        ),
        in_specs=[whole()],
        out_specs=(whole(), whole()),
        compiler_params=PARAMS,
        name="join",
    )(incoming)
    return (grad_in.reshape(1, 1, 64, 1, 256), gain_grad.reshape(512))


def solution(mesh):
    fine = Mesh(mesh.devices.reshape(2, 4, 4, 8, 2), ("zh", "y", "x", "zl", "c"))
    dp, shard = ("zh", "y"), ("x", "zl", "c")
    return jax.shard_map(
        shards,
        mesh=fine,
        in_specs=(
            P(dp, None, shard, None, None),
            P(dp, None, shard, None, None),
            P(),
            P(shard, None, None),
            P(shard, None, None),
        ),
        out_specs=(P(dp, shard, None, None, None), P()),
        check_vma=False,
    )
```

time: 430 us -> 137 us (0.32)
  the two profiles are of different devices: /device:TPU:2 before, /device:TPU:1 now
where the time goes in v1:
time: 137 us
  blocking collectives  53.4 us (39%)
  starting transfers between devices  41.3 us (30%)
  between operations  14.2 us (10%)
  waiting for transfers between devices  14.1 us (10%)
  Pallas kernels  7.87 us (6%)
  local copies, waits for them, and re-layouts  5.33 us (4%)
    all_to_all x1, blocking collectives, shards(): lax.all_to_all(outgoing, shard, split_axis=0, concat_axis=0, tiled=True)  23.3 us
    ppermute x3, starting transfers between devices, shards(): gain_terms = gain_terms + lax.ppermute(gain_terms, axis, pairs)  20.1 us
    all_gather x1, blocking collectives, shards(): gathered = lax.all_gather(grads, group, axis=0)  15.9 us
    all_gather x1, blocking collectives, shards(): high_all = lax.all_gather(jnp.concatenate([near, far], axis=1), 'y', axis=0)  14.2 us
    all_to_all x1, starting transfers between devices, shards(): lax.all_to_all(jnp.broadcast_to(chunk[None], (8, 512, 256)), group, split...  13.7 us
    ppermute x1, waiting for transfers between devices, shards(): far = lax.ppermute(high, ring, ring_pairs(FAR))  9.18 us
    ppermute x1, starting transfers between devices, shards(): halo = lax.ppermute(edge, shard, halo_pairs)  4.94 us
    pallas_call x1, Pallas kernels, shards(): pl.pallas_call(high_kernel_body, out_shape=(jax.ShapeDtypeStruct((256, 12...  3.98 us
  transfers between devices with their start and end apart: 8, of which 4 were waited for; matrix products, arithmetic and copies ran while one was open for 1% of the time, Pallas kernels for 3%

profile of v1, /device:TPU:1, one launch (start us, length us, event | category | flops | bytes accessed | tf_op | source)
XLA Modules:
  0.0 136.5 jit_solution(6737567808097294471)
XLA Ops:
  7.2 0.9 copy.16
  8.1 4.9 %collective-permute-start = (bf16[16,8,256]{2,1,0:T(8,128)(2,1)S(1)}, bf16[16,8,256]{2,1,0:T(8,128)(2,1)S(1)}, u32[]{:S(2)}, u32[]{:S(2)}) collective-permute-start(bf16[16,8,256]{2,1,0:T(8,128)(2,1)S(1)} %fusion), channel_id=1, source_target_pairs={{2,1},{4,3},{6,5},{8,7},{10,9},{12,11},{14,13},{16,15},{18,17},{20... | collective-permute-start | bytes 196616 | tf_op jit(solution)/shard_map/ppermute | solution.py:265
  13.1 0.9 reshape.31
  13.9 1.1 collective-permute-done
  15.1 1.5 %broadcast_in_dim.7 = bf16[8,512,256]{2,1,0:T(8,128)(2,1)} broadcast(bf16[512,256]{1,0:T(8,128)(2,1)S(1)} %pad_maximum_fusion), dimensions={1,2} | broadcast | bytes 2359296 | tf_op jit(solution)/shard_map/broadcast_in_dim | solution.py:281
  16.6 13.7 %all-to-all-start = ((bf16[8,512,256]{2,1,0:T(8,128)(2,1)}), bf16[8,512,256]{2,1,0:T(8,128)(2,1)S(1)}, u32[]{:S(2)}, u32[]{:S(2)}) async-start(bf16[8,512,256]{2,1,0:T(8,128)(2,1)} %broadcast_in_dim.7), calls=%async_computation | async-start | bytes 4194304 | tf_op jit(solution)/shard_map/all_to_all | solution.py:280
  30.4 0.7 all_gather_reshape.3
  31.1 1.9 %collective-permute-start.2 = (bf16[27,8,256]{2,1,0:T(8,128)(2,1)S(1)}, bf16[27,8,256]{2,1,0:T(8,128)(2,1)S(1)}, u32[]{:S(2)}, u32[]{:S(2)}) collective-permute-start(bf16[27,8,256]{2,1,0:T(8,128)(2,1)S(1)} %bitcast.31), channel_id=1, source_target_pairs={{8,0},{265,1},{10,2},{267,3},{12,4},{269,5},{14,6},{271,7},{256,8}... | collective-permute-start | bytes 331784 | tf_op jit(solution)/shard_map/ppermute | solution.py:269
  33.0 0.7 collective-permute-start.1
  33.7 0.1 pad_add_fusion.place_ref
  33.8 9.2 %collective-permute-done.2 = bf16[27,8,256]{2,1,0:T(8,128)(2,1)S(1)} collective-permute-done((bf16[27,8,256]{2,1,0:T(8,128)(2,1)S(1)}, bf16[27,8,256]{2,1,0:T(8,128)(2,1)S(1)}, u32[]{:S(2)}, u32[]{:S(2)}) %collective-permute-start.2) | collective-permute-done | bytes 110624 | tf_op jit(solution)/shard_map/ppermute | solution.py:269
  43.0 14.2 %all-gather = bf16[108,16,256]{2,1,0:T(8,128)(2,1)S(1)} all-gather(bf16[27,16,256]{2,1,0:T(8,128)(2,1)S(1)} %pad_maximum_fusion.1), channel_id=2, replica_groups=mesh['zh'=2,'y'=4,'x'=4,'zl'=8,'c'=2] {'y'}, dimensions={0}, use_global_device_ids=true | all-gather | bytes 1105920 | tf_op jit(solution)/shard_map/all_gather | solution.py:283
  57.2 4.0 %high_conv.1 = (bf16[256,128]{1,0:T(8,128)(2,1)S(1)}, f32[8,128]{1,0:T(8,128)S(1)}) custom-call(s32[3]{0:T(128)S(1)} %pad_add_fusion.place_ref, bf16[8,512,256]{2,1,0:T(8,128)(2,1)S(1)} %all-to-all-done.parts_ref, bf16[4,27,16,256]{3,2,1,0:T(8,128)(2,1)S(1)} %bitcast.23, f32[1,512]{1,0:T(1,128)S(1)} %bitcast.25), custom_call_target="tpu_custom_call" | custom-call | tf_op jit(solution)/shard_map/high_conv/pallas_call | solution.py:285
  61.2 2.6 %collective-permute-start.3 = (f32[8,128]{1,0:T(8,128)S(1)}, f32[8,128]{1,0:T(8,128)S(1)}, u32[]{:S(2)}, u32[]{:S(2)}) collective-permute-start(f32[8,128]{1,0:T(8,128)S(1)} %get-tuple-element.6), channel_id=1, source_target_pairs={{0,64},{64,0},{128,192},{192,128},{1,65},{65,1},{129,193},{193,129... | collective-permute-start | bytes 12296 | tf_op jit(solution)/shard_map/ppermute | solution.py:304
  63.8 2.2 %collective-permute-done.3 = f32[8,128]{1,0:T(8,128)S(1)} collective-permute-done((f32[8,128]{1,0:T(8,128)S(1)}, f32[8,128]{1,0:T(8,128)S(1)}, u32[]{:S(2)}, u32[]{:S(2)}) %collective-permute-start.3) | collective-permute-done | bytes 4128 | tf_op jit(solution)/shard_map/ppermute | solution.py:304
  66.0 4.2 %collective-permute-start.4 = (f32[8,128]{1,0:T(8,128)S(1)}, f32[8,128]{1,0:T(8,128)S(1)}, u32[]{:S(2)}, u32[]{:S(2)}) collective-permute-start(f32[8,128]{1,0:T(8,128)S(1)} %add.11), channel_id=1, source_target_pairs={{0,128},{64,192},{128,0},{192,64},{1,129},{65,193},{129,1},{193,65... | collective-permute-start | bytes 12296 | tf_op jit(solution)/shard_map/ppermute | solution.py:304
  70.2 1.7 %collective-permute-done.4 = f32[8,128]{1,0:T(8,128)S(1)} collective-permute-done((f32[8,128]{1,0:T(8,128)S(1)}, f32[8,128]{1,0:T(8,128)S(1)}, u32[]{:S(2)}, u32[]{:S(2)}) %collective-permute-start.4) | collective-permute-done | bytes 4128 | tf_op jit(solution)/shard_map/ppermute | solution.py:304
  71.8 13.3 %collective-permute-start.5 = (f32[8,128]{1,0:T(8,128)S(1)}, f32[8,128]{1,0:T(8,128)S(1)}, u32[]{:S(2)}, u32[]{:S(2)}) collective-permute-start(f32[8,128]{1,0:T(8,128)S(1)} %add.12), channel_id=1, source_target_pairs={{0,256},{256,0},{1,257},{257,1},{2,258},{258,2},{3,259},{259,3},{4... | collective-permute-start | bytes 12296 | tf_op jit(solution)/shard_map/ppermute | solution.py:304
  85.2 15.9 %all-gather.1 = bf16[2048,128]{1,0:T(8,128)(2,1)S(1)} all-gather(bf16[256,128]{1,0:T(8,128)(2,1)S(1)} %get-tuple-element.7), channel_id=3, replica_groups=mesh['zh'=2,'y'=4,'x'=4,'zl'=8,'c'=2] {'x','c'}, dimensions={0}, use_global_device_ids=true | all-gather | bytes 589824 | tf_op jit(solution)/shard_map/all_gather | solution.py:298
  101.1 1.3 copy-done
  102.4 2.7 %low_conv.1 = bf16[64,8,128]{2,1,0:T(8,128)(2,1)S(1)} custom-call(s32[3]{0:T(128)S(1)} %pad_add_fusion.place_ref, bf16[8,256,128]{2,1,0:T(8,128)(2,1)S(1)} %bitcast.24, bf16[8,512,256]{2,1,0:T(8,128)(2,1)S(1)} %all-to-all-done.parts_ref, bf16[8,144,512]{2,1,0:T(8,128)(2,1)S(1)} %copy-done), custom_call_target="tpu_custom_call" | custom-call | tf_op jit(solution)/shard_map/low_conv/pallas_call | solution.py:306
  105.0 0.1 broadcast_select_fusion
  105.1 23.3 %all_to_all.10.refs_0_ = bf16[64,8,128]{2,1,0:T(8,128)(2,1)S(1)} all-to-all(bf16[64,8,128]{2,1,0:T(8,128)(2,1)S(1)} %broadcast_select_fusion), channel_id=1, replica_groups=mesh['zh'=2,'y'=4,'x'=4,'zl'=8,'c'=2] {'x','zl','c'}, dimensions={0} | all-to-all | bytes 262144 | tf_op jit(solution)/shard_map/all_to_all | solution.py:321
  128.4 1.2 join.1
  (25 shorter events, 0.3 us)
Async XLA Ops:
  8.1 6.9 %collective-permute-start = (bf16[16,8,256]{2,1,0:T(8,128)(2,1)S(1)}, bf16[16,8,256]{2,1,0:T(8,128)(2,1)S(1)}, u32[]{:S(2)}, u32[]{:S(2)}) collective-permute-start(bf16[16,8,256]{2,1,0:T(8,128)(2,1)S(1)} %fusion), channel_id=1, source_target_pairs={{2,1},{4,3},{6,5},{8,7},{10,9},{12,11},{14,13},{16,15},{18,17},{20... | collective-permute-start | bytes 196616 | tf_op jit(solution)/shard_map/ppermute | solution.py:265
  16.6 13.7 %copy-start.2 = (bf16[4,27,512]{2,0,1:T(4,128)(2,1)S(1)}, bf16[4,27,512]{2,0,1:T(4,128)(2,1)}, u32[]{:S(2)}) copy-start(bf16[4,27,512]{2,0,1:T(4,128)(2,1)} %param.9) | copy-start | bytes 331780
  16.6 14.5 %copy-start.3 = (bf16[8,27,256]{2,0,1:T(8,128)(2,1)S(1)}, bf16[8,27,256]{2,0,1:T(8,128)(2,1)}, u32[]{:S(2)}) copy-start(bf16[8,27,256]{2,0,1:T(8,128)(2,1)} %param.8) | copy-start | bytes 331780
  16.6 40.7 %all-to-all-start = ((bf16[8,512,256]{2,1,0:T(8,128)(2,1)}), bf16[8,512,256]{2,1,0:T(8,128)(2,1)S(1)}, u32[]{:S(2)}, u32[]{:S(2)}) async-start(bf16[8,512,256]{2,1,0:T(8,128)(2,1)} %broadcast_in_dim.7), calls=%async_computation | async-start | bytes 4194304 | tf_op jit(solution)/shard_map/all_to_all | solution.py:280
  30.3 27.0 %copy-start.1 = (f32[512]{0:T(512)S(1)}, f32[512]{0:T(512)}, u32[]{:S(2)}) copy-start(f32[512]{0:T(512)} %param.7) | copy-start | bytes 6148
  30.3 70.8 %all-gather.4.cloned.1.call-start = ((), (), s32[]{:S(2)}) async-start(), calls=%async_computation.2 | async-start | bytes 1327104 | tf_op jit(solution)/shard_map/all_gather | solution.py:260
  31.1 11.9 %collective-permute-start.2 = (bf16[27,8,256]{2,1,0:T(8,128)(2,1)S(1)}, bf16[27,8,256]{2,1,0:T(8,128)(2,1)S(1)}, u32[]{:S(2)}, u32[]{:S(2)}) collective-permute-start(bf16[27,8,256]{2,1,0:T(8,128)(2,1)S(1)} %bitcast.31), channel_id=1, source_target_pairs={{8,0},{265,1},{10,2},{267,3},{12,4},{269,5},{14,6},{271,7},{256,8}... | collective-permute-start | bytes 331784 | tf_op jit(solution)/shard_map/ppermute | solution.py:269
  33.0 9.9 %collective-permute-start.1 = (bf16[27,8,256]{2,1,0:T(8,128)(2,1)S(1)}, bf16[27,8,256]{2,1,0:T(8,128)(2,1)S(1)}, u32[]{:S(2)}, u32[]{:S(2)}) collective-permute-start(bf16[27,8,256]{2,1,0:T(8,128)(2,1)S(1)} %bitcast.32), channel_id=1, source_target_pairs={{0,0},{1,1},{2,2},{3,3},{4,4},{5,5},{6,6},{7,7},{8,8},{9,9},{10,10... | collective-permute-start | bytes 331784 | tf_op jit(solution)/shard_map/ppermute | solution.py:268
  61.2 4.8 %collective-permute-start.3 = (f32[8,128]{1,0:T(8,128)S(1)}, f32[8,128]{1,0:T(8,128)S(1)}, u32[]{:S(2)}, u32[]{:S(2)}) collective-permute-start(f32[8,128]{1,0:T(8,128)S(1)} %get-tuple-element.6), channel_id=1, source_target_pairs={{0,64},{64,0},{128,192},{192,128},{1,65},{65,1},{129,193},{193,129... | collective-permute-start | bytes 12296 | tf_op jit(solution)/shard_map/ppermute | solution.py:304
  66.0 5.8 %collective-permute-start.4 = (f32[8,128]{1,0:T(8,128)S(1)}, f32[8,128]{1,0:T(8,128)S(1)}, u32[]{:S(2)}, u32[]{:S(2)}) collective-permute-start(f32[8,128]{1,0:T(8,128)S(1)} %add.11), channel_id=1, source_target_pairs={{0,128},{64,192},{128,0},{192,64},{1,129},{65,193},{129,1},{193,65... | collective-permute-start | bytes 12296 | tf_op jit(solution)/shard_map/ppermute | solution.py:304
  71.8 29.2 %collective-permute-start.5 = (f32[8,128]{1,0:T(8,128)S(1)}, f32[8,128]{1,0:T(8,128)S(1)}, u32[]{:S(2)}, u32[]{:S(2)}) collective-permute-start(f32[8,128]{1,0:T(8,128)S(1)} %add.12), channel_id=1, source_target_pairs={{0,256},{256,0},{1,257},{257,1},{2,258},{258,2},{3,259},{259,3},{4... | collective-permute-start | bytes 12296 | tf_op jit(solution)/shard_map/ppermute | solution.py:304
  101.1 1.3 copy-start
Sparse Core Ops, SparseCore 0:
  33.2 64.1 all-gather.3

commit v2 on v1

--- a/solution.py
+++ b/solution.py
@@ -11,9 +11,8 @@
 EPSILON = 1e-06
 F32 = jnp.float32
 BF16 = jnp.bfloat16
-NEAR = (0, 1, -1, 2)
-FAR = (4, -3, 3, -2)
-OFFSETS = tuple(o for pair in zip(NEAR, FAR) for o in pair)
+NEAR = ((0, 1, -1, 2), (0, -1, 1, 2))
+FAR = ((4, -3, 3, -2), (-4, 3, -3, -2))
 NT = (((1,), (1,)), ((), ()))
 
 
@@ -21,11 +20,23 @@
     return lax.broadcasted_iota(jnp.int32, shape, dim)
 
 
-def owner_z(slot, z):
+def owner_z(slot, z, c):
     offset = jnp.zeros_like(slot)
-    for n, o in enumerate(OFFSETS):
-        offset = jnp.where(slot == n, o % 8, offset)
+    for y in range(4):
+        for n, table in enumerate((NEAR, FAR)):
+            by = jnp.where(c == 0, table[0][y] % 8, table[1][y] % 8)
+            offset = jnp.where(slot == 2 * y + n, by, offset)
     return (z + offset) & 7
+
+
+def slot_of(owner, z, c):
+    distance = (owner - z) & 7
+    slot = jnp.int32(0)
+    for y in range(4):
+        for n, table in enumerate((NEAR, FAR)):
+            by = jnp.where(c == 0, table[0][y] % 8, table[1][y] % 8)
+            slot = jnp.where(distance == by, 2 * y + n, slot)
+    return slot
 
 
 def row_shift(value, by):
@@ -46,6 +57,24 @@
 
 def inverse_rms(mid):
     return lax.rsqrt(jnp.mean(mid * mid, axis=1, keepdims=True) + EPSILON)
+
+
+def pack_body(place_ref, rows_ref, halo_ref, mid_ref, out_ref):
+    c = place_ref[1]
+    for core in range(2):
+
+        @pl.when(c == core)
+        def _():
+            for n in range(8):
+                if core == 0:
+                    block = (halo_ref[...], rows_ref[:, 0], rows_ref[:, 1])
+                else:
+                    block = (rows_ref[:, 0], rows_ref[:, 1], halo_ref[...])
+                for r in range(3):
+                    out_ref[n, r] = block[r]
+
+    for n in range(8):
+        out_ref[n, 3] = mid_ref[...]
 
 
 def high_kernel_body(place_ref, parts_ref, weight_ref, gain_ref, out_ref, gain_out_ref, taps_ref, wide_ref):
@@ -56,7 +85,7 @@
                 tap = 9 * (2 - dt) + 3 * (2 - dy) + dw
                 for j in range(4):
                     at = (dw * 4 + dt) * 64 + 16 * j
-                    taps_ref[dy, at : at + 16, :] = weight_ref[j, tap]
+                    taps_ref[dy, at : at + 16, :] = weight_ref[j, 16 * tap : 16 * tap + 16, :]
             at = (dw * 4 + 3) * 64
             taps_ref[dy, at : at + 64, :] = jnp.zeros((64, 256), BF16)
     row = iota((256, 256), 0)
@@ -92,7 +121,7 @@
     )
     lane = iota((1, 128), 1)
     slot = (lane >> 3) & 7
-    target = 128 * x + 16 * owner_z(slot, z) + 8 * c + (lane & 7)
+    target = 128 * x + 16 * owner_z(slot, z, c) + 8 * c + (lane & 7)
     channel = iota((512, 128), 0)
     hit = channel == target
     half = iota((512, 128), 1) >> 6
@@ -115,26 +144,28 @@
     normed = scaled * gain
     gate = jax.nn.sigmoid(normed)
     grad = summed * (gate * (1.0 + normed * (1.0 - gate)))
-    out_ref[...] = (grad * gain).astype(BF16)
+    sent = (grad * gain).astype(BF16)
+    out_ref[...] = sent
     terms = jnp.sum(grad * scaled, axis=0, keepdims=True)
     terms = terms + half_turn(terms)
     source = iota((128, 128), 0)
-    place = (source & 64) + 8 * owner_z((source >> 3) & 7, z) + (source & 7)
+    place = (source & 64) + 8 * owner_z((source >> 3) & 7, z, c) + (source & 7)
     order = jnp.where(place == iota((128, 128), 1), 1.0, 0.0)
-    gain_out_ref[...] = jnp.dot(
+    terms = jnp.dot(
         jnp.broadcast_to(terms, (8, 128)),
         order,
         precision=lax.Precision.HIGHEST,
         preferred_element_type=F32,
     )
+    gain_out_ref[...] = terms
 
 
 def low_kernel_body(place_ref, grads_ref, parts_ref, weight_ref, out_ref, turned_ref):
-    z = place_ref[2]
+    c, z = place_ref[1], place_ref[2]
     source = iota((256, 256), 0)
     target = (
         ((source >> 6) & 1) * 128
-        + owner_z((source >> 3) & 7, z) * 16
+        + owner_z((source >> 3) & 7, z, source >> 7) * 16
         + (source >> 7) * 8
         + (source & 7)
     )
@@ -162,23 +193,46 @@
     frame = (row >> 2) & 15
     column = row & 3
     total = jnp.zeros((512, 128), F32)
+    slots = [slot_of(n, z, c) for n in range(8)]
     for a in range(3):
-        for c in range(3):
-            at = 16 * (3 * a + c)
-            taps = jnp.concatenate([weight_ref[n, at : at + 16, :] for n in range(8)], axis=0)
+        for b in range(3):
+            at = 16 * (3 * a + b)
+            taps = jnp.concatenate(
+                [
+                    jnp.concatenate(
+                        [weight_ref[n, at : at + 16, :], weight_ref[n, 144 + at : 160 + at, :]],
+                        axis=1,
+                    )
+                    for n in slots
+                ],
+                axis=0,
+            )
             product = lax.dot_general(grads, taps, NT, preferred_element_type=F32)
-            moved = row_shift(product, 4 * (2 - a) + 1 - c)
-            keep = (frame + 2 - a < 16) & (column + 1 - c >= 0) & (column + 1 - c < 4)
+            moved = row_shift(product, 4 * (2 - a) + 1 - b)
+            keep = (frame + 2 - a < 16) & (column + 1 - b >= 0) & (column + 1 - b < 4)
             total = total + jnp.where(keep, moved, 0.0)
     result = total[0:256] + pltpu.roll(total[256:512], 4, 1)
     for pair in range(4):
         turned_ref[:, pair, :] = result[64 * pair : 64 * pair + 64]
-    turned_ref[:, 4:8, :] = jnp.zeros((64, 4, 128), F32)
     out_ref[...] = turned_ref[...].astype(BF16)
 
 
-def join_body(scale, parts_ref, out_ref, gain_ref):
-    parts = parts_ref[...].astype(F32)
+def close_body(rows_ref, terms_ref, out_ref):
+    terms = terms_ref[0]
+    for n in range(1, 4):
+        terms = terms + terms_ref[n]
+    head = terms.astype(BF16).astype(F32)
+    line = jnp.where(iota((8, 128), 1) < 64, head, terms - head)[0:2].astype(BF16)
+    out_ref[:, 0] = rows_ref[:, 0:2]
+    out_ref[:, 1] = rows_ref[:, 2:4]
+    out_ref[:, 2] = jnp.broadcast_to(line[None], (64, 2, 128))
+
+
+def join_body(scale, parts_ref, out_ref, gain_ref, rows_ref):
+    for n in range(3):
+        rows_ref[:, 2 * n : 2 * n + 2, :] = parts_ref[:, n].astype(F32)
+    rows_ref[:, 6:8, :] = jnp.zeros((64, 2, 128), F32)
+    parts = rows_ref[...]
     strips = [
         jnp.concatenate([parts[16 * x + 2 * z + c] for z in range(8)], axis=0)
         for x in range(4)
@@ -239,10 +293,7 @@
         for y in range(4):
             for zl in range(8):
                 for c in range(2):
-                    by = distances[y]
-                    if by == 4 and c == 1:
-                        by = -4
-                    at = (zh * 8 + zl + by) % 16
+                    at = (zh * 8 + zl + distances[c][y]) % 16
                     source = ((at // 8 * 4 + y) * 8 + at % 8) * 2 + c
                     pairs.append((source, ((zh * 4 + y) * 8 + zl) * 2 + c))
     return pairs
@@ -255,32 +306,33 @@
     group = ("x", "c")
     shard = ("x", "zl", "c")
 
-    low = jnp.transpose(low_kernel.reshape(4, 3, 3, 3, 512), (1, 3, 2, 0, 4))
-    low = jnp.pad(low, ((0, 0), (0, 0), (0, 1), (0, 0), (0, 0))).reshape(144, 512)
-    low_all = lax.all_gather(low, "zl", axis=0)
-
     grad = grad_out[0]
     edge = jnp.where(c == 0, grad[:, 0], grad[:, 1])
     halo_pairs = [(s, s - 1) for s in range(2, 64, 2)] + [(s, s + 1) for s in range(1, 62, 2)]
     halo = lax.ppermute(edge, shard, halo_pairs)
 
-    high = jnp.transpose(high_kernel, (1, 0, 2))
-    near = lax.ppermute(high, ring, ring_pairs(NEAR))
-    far = lax.ppermute(high, ring, ring_pairs(FAR))
-
-    own = jnp.transpose(grad, (1, 0, 2, 3)).reshape(256, 256)
-    halo = halo.reshape(128, 256)
-    rows = jnp.where(
-        c == 0,
-        jnp.concatenate([halo, own], axis=0),
-        jnp.concatenate([own, halo], axis=0),
-    )
+    high = jnp.transpose(high_kernel, (1, 0, 2)).reshape(216, 256)
+    low = jnp.transpose(low_kernel.reshape(4, 3, 3, 3, 2, 256), (4, 1, 3, 2, 0, 5))
+    low = jnp.pad(low, ((0, 0), (0, 0), (0, 0), (0, 1), (0, 0), (0, 0))).reshape(288, 256)
+    kernels = jnp.concatenate([high, low], axis=0)
+    near = lax.ppermute(kernels, ring, ring_pairs(NEAR))
+    far = lax.ppermute(kernels, ring, ring_pairs(FAR))
+
     mid = saved_mid.reshape(64, 512)
-    chunk = jnp.concatenate([rows, mid[:, 0:256], mid[:, 256:512]], axis=0)
-    parts = lax.all_to_all(
-        jnp.broadcast_to(chunk[None], (8, 512, 256)), group, split_axis=0, concat_axis=0, tiled=True
-    )
-    high_all = lax.all_gather(jnp.concatenate([near, far], axis=1), "y", axis=0)
+    mid = jnp.concatenate([mid[:, 0:256], mid[:, 256:512]], axis=0).reshape(16, 8, 256)
+    packed = pl.pallas_call(
+        pack_body,
+        out_shape=jax.ShapeDtypeStruct((8, 4, 16, 8, 256), BF16),
+        in_specs=[scalars()] + [whole()] * 3,
+        out_specs=whole(),
+        compiler_params=PARAMS,
+        name="pack_rows",
+    )(place, grad, halo, mid)
+    parts = lax.all_to_all(packed.reshape(8, 512, 256), group, split_axis=0, concat_axis=0, tiled=True)
+    high = jnp.concatenate([near[:216].reshape(27, 8, 256), far[:216].reshape(27, 8, 256)], axis=1)
+    high_all = lax.all_gather(high.reshape(432, 256), "y", axis=0)
+    low = jnp.stack([near[216:], far[216:]], axis=0)
+    low_all = lax.all_gather(low, "y", axis=0, tiled=True)
 
     grads, gain_terms = pl.pallas_call(
         high_kernel_body,
@@ -295,29 +347,33 @@
         name="high_conv",
     )(place, parts, high_all, norm_gain.reshape(1, 512))
 
+    halves = [(z, (z + 4) % 16 if z % 8 >= 4 else (z - 4) % 16) for z in range(16)]
+    other = lax.ppermute(gain_terms, ("zh", "zl"), halves)
     gathered = lax.all_gather(grads, group, axis=0)
-    for axis, pairs in (
-        ("y", [(i, i ^ 1) for i in range(4)]),
-        ("y", [(i, i ^ 2) for i in range(4)]),
-        ("zh", [(0, 1), (1, 0)]),
-    ):
-        gain_terms = gain_terms + lax.ppermute(gain_terms, axis, pairs)
+    other, gathered = lax.optimization_barrier((other, gathered))
+    clips = lax.all_to_all(
+        jnp.broadcast_to((gain_terms + other)[None], (4, 8, 128)), "y", split_axis=0, concat_axis=0, tiled=True
+    )
 
     partial = pl.pallas_call(
         low_kernel_body,
-        out_shape=jax.ShapeDtypeStruct((64, 8, 128), BF16),
+        out_shape=jax.ShapeDtypeStruct((64, 4, 128), BF16),
         in_specs=[scalars(), whole(), whole(), whole()],
         out_specs=whole(),
-        scratch_shapes=[pltpu.VMEM((64, 8, 128), F32)],
+        scratch_shapes=[pltpu.VMEM((64, 4, 128), F32)],
         compiler_params=PARAMS,
         name="low_conv",
     )(place, gathered, parts, low_all)
 
-    head = lax.reduce_precision(gain_terms, 8, 7)
-    tail = gain_terms - head
-    line = jnp.where(lax.broadcasted_iota(jnp.int32, (8, 128), 1) < 64, head, tail).astype(BF16)
-    is_gain = lax.broadcasted_iota(jnp.int32, (64, 8, 128), 1) == 4
-    outgoing = jnp.where(is_gain, line[None], partial)
+    outgoing = pl.pallas_call(
+        close_body,
+        out_shape=jax.ShapeDtypeStruct((64, 3, 2, 128), BF16),
+        in_specs=[whole(), whole()],
+        out_specs=whole(),
+        compiler_params=PARAMS,
+        name="close",
+    )(partial, clips)
+    outgoing = outgoing.reshape(192, 2, 128)
     incoming = lax.all_to_all(outgoing, shard, split_axis=0, concat_axis=0, tiled=True)
 
     positions = 8 * 16 * 128 * 8
@@ -329,9 +385,10 @@
         ),
         in_specs=[whole()],
         out_specs=(whole(), whole()),
+        scratch_shapes=[pltpu.VMEM((64, 8, 128), F32)],
         compiler_params=PARAMS,
         name="join",
-    )(incoming)
+    )(incoming.reshape(64, 3, 2, 128))
     return (grad_in.reshape(1, 1, 64, 1, 256), gain_grad.reshape(512))
 
 

time: 137 us -> 136 us (level)
  starting transfers between devices: 41.3 us -> 31.8 us
  waiting for transfers between devices: 14.1 us -> 21.4 us
  blocking collectives: 53.4 us -> 51.3 us
  other arithmetic: 0.29 us -> 1.79 us
    ppermute x5 -> x3, waiting for transfers between devices: 13 us -> 0.01 us  [the longest x1 0.01 us: shards(): far = lax.ppermute(kernels, ring, ring_pairs(FAR))]
    all_to_all x1 -> x2, waiting for transfers between devices: 0.01 us -> 13 us  [the longest x1 12.7 us: shards(): lax.all_to_all(packed.reshape(8, 512, 256), group, split_axis=0, concat_a...]
    ppermute x5 -> x3, starting transfers between devices: 22.6 us -> 12.4 us  [the longest x1 9.65 us: shards(): far = lax.ppermute(kernels, ring, ring_pairs(FAR))]
    ppermute x1, waiting for transfers between devices: 1.06 us -> 8.41 us  [shards(): halo = lax.ppermute(edge, shard, halo_pairs)]
    ppermute x1, starting transfers between devices: 4.94 us -> 7.13 us  [shards(): halo = lax.ppermute(edge, shard, halo_pairs)]
    all_gather x1, blocking collectives: 15.9 us -> 14.1 us  [shards(): gathered = lax.all_gather(grads, group, axis=0)]
    all_gather x1, blocking collectives: 14.2 us -> 12.7 us  [shards(): high_all = lax.all_gather(high.reshape(432, 256), 'y', axis=0)]
    all_to_all x1 -> x2, starting transfers between devices: 13.7 us -> 12.3 us  [the longest x1 7.32 us: shards(): lax.all_to_all(packed.reshape(8, 512, 256), group, split_axis=0, concat_a...]
  transfers between devices with their start and end apart: 8 -> 7, of which waited for: 4 -> 3; matrix products, arithmetic and copies ran while one was open for 1% -> 2% of each run, Pallas kernels for 3% -> 5%
where the time goes in v2:
time: 136 us; the launch traced here: 135 us
  blocking collectives  51.3 us (38%)
  starting transfers between devices  31.8 us (23%)
  waiting for transfers between devices  21.4 us (16%)
  between operations  14.2 us (10%)
  Pallas kernels  8.68 us (6%)
  local copies, waits for them, and re-layouts  6.17 us (5%)
  other arithmetic  1.79 us (1%)
    all_to_all x1, blocking collectives, shards(): lax.all_to_all(outgoing, shard, split_axis=0, concat_axis=0, tiled=True)  24.4 us
    all_gather x1, blocking collectives, shards(): gathered = lax.all_gather(grads, group, axis=0)  14.1 us
    all_gather x1, blocking collectives, shards(): high_all = lax.all_gather(high.reshape(432, 256), 'y', axis=0)  12.7 us
    all_to_all x1, waiting for transfers between devices, shards(): lax.all_to_all(packed.reshape(8, 512, 256), group, split_axis=0, concat_a...  12.7 us
    ppermute x1, starting transfers between devices, shards(): far = lax.ppermute(kernels, ring, ring_pairs(FAR))  9.65 us
    ppermute x1, waiting for transfers between devices, shards(): halo = lax.ppermute(edge, shard, halo_pairs)  8.41 us
    all_to_all x1, starting transfers between devices, shards(): lax.all_to_all(packed.reshape(8, 512, 256), group, split_axis=0, concat_a...  7.32 us
    ppermute x1, starting transfers between devices, shards(): halo = lax.ppermute(edge, shard, halo_pairs)  7.13 us
  transfers between devices with their start and end apart: 7, of which 3 were waited for; matrix products, arithmetic and copies ran while one was open for 2% of the time, Pallas kernels for 5%

profile of v2, /device:TPU:1, one launch (start us, length us, event | category | flops | bytes accessed | tf_op | source)
XLA Modules:
  0.0 135.3 jit_solution(955366804547908613)
XLA Ops:
  7.2 1.0 reshape.50
  8.3 0.9 pad_maximum_fusion.1
  9.2 9.6 %collective-permute-start.2 = (bf16[504,256]{1,0:T(8,128)(2,1)S(1)}, bf16[504,256]{1,0:T(8,128)(2,1)S(1)}, u32[]{:S(2)}, u32[]{:S(2)}) collective-permute-start(bf16[504,256]{1,0:T(8,128)(2,1)S(1)} %pad_maximum_fusion.1), channel_id=1, source_target_pairs={{8,0},{265,1},{10,2},{267,3},{12,4},{269,5},{14,6},{271,7},{256,8}... | collective-permute-start | bytes 774152 | tf_op jit(solution)/shard_map/ppermute | solution.py:319
  18.9 0.7 collective-permute-start.1
  19.6 0.9 copy.16
  20.5 7.1 %collective-permute-start = (bf16[16,8,256]{2,1,0:T(8,128)(2,1)S(1)}, bf16[16,8,256]{2,1,0:T(8,128)(2,1)S(1)}, u32[]{:S(2)}, u32[]{:S(2)}) collective-permute-start(bf16[16,8,256]{2,1,0:T(8,128)(2,1)S(1)} %fusion), channel_id=1, source_target_pairs={{2,1},{4,3},{6,5},{8,7},{10,9},{12,11},{14,13},{16,15},{18,17},{20... | collective-permute-start | bytes 196616 | tf_op jit(solution)/shard_map/ppermute | solution.py:312
  27.7 0.9 reshape.46
  28.6 8.4 %collective-permute-done.halo_ref = bf16[16,8,256]{2,1,0:T(8,128)(2,1)S(1)} collective-permute-done((bf16[16,8,256]{2,1,0:T(8,128)(2,1)S(1)}, bf16[16,8,256]{2,1,0:T(8,128)(2,1)S(1)}, u32[]{:S(2)}, u32[]{:S(2)}) %collective-permute-start) | collective-permute-done | bytes 65568 | tf_op jit(solution)/shard_map/ppermute | solution.py:312
  37.0 0.7 pack_rows.1
  37.7 1.3 copy-done
  39.1 7.3 %all-to-all-start = ((bf16[8,512,256]{2,1,0:T(8,128)(2,1)}), bf16[8,512,256]{2,1,0:T(8,128)(2,1)S(1)}, u32[]{:S(2)}, u32[]{:S(2)}) async-start(bf16[8,512,256]{2,1,0:T(8,128)(2,1)} %bitcast.35), calls=%async_computation | async-start | bytes 4194304 | tf_op jit(solution)/shard_map/all_to_all | solution.py:331
  46.5 0.8 pad_maximum_fusion
  47.3 12.7 %all_gather.12.weight_ref = bf16[4,432,256]{2,1,0:T(8,128)(2,1)S(1)} all-gather(bf16[1,432,256]{2,1,0:T(8,128)(2,1)S(1)} %bitcast.41), channel_id=1, replica_groups=mesh['zh'=2,'y'=4,'x'=4,'zl'=8,'c'=2] {'y'}, dimensions={0}, use_global_device_ids=true | all-gather | bytes 1105920 | tf_op jit(solution)/shard_map/all_gather | solution.py:333
  60.0 12.7 %all-to-all-done.parts_ref = bf16[8,512,256]{2,1,0:T(8,128)(2,1)S(1)} async-done(((bf16[8,512,256]{2,1,0:T(8,128)(2,1)}), bf16[8,512,256]{2,1,0:T(8,128)(2,1)S(1)}, u32[]{:S(2)}, u32[]{:S(2)}) %all-to-all-start) | async-done | bytes 2097184 | tf_op jit(solution)/shard_map/all_to_all | solution.py:331
  72.7 3.9 %high_conv.1 = (bf16[256,128]{1,0:T(8,128)(2,1)S(1)}, f32[8,128]{1,0:T(8,128)S(1)}) custom-call(s32[3]{0:T(128)S(1)} %pad_add_fusion.place_ref, bf16[8,512,256]{2,1,0:T(8,128)(2,1)S(1)} %all-to-all-done.parts_ref, bf16[4,432,256]{2,1,0:T(8,128)(2,1)S(1)} %all_gather.12.weight_ref, f32[1,512]{1,0:T(1,128)S(1)} %bitcast.40), custom_call_target="tpu_custom_call" | custom-call | tf_op jit(solution)/shard_map/high_conv/pallas_call | solution.py:337
  76.7 2.1 %collective-permute-start.3 = (f32[8,128]{1,0:T(8,128)S(1)}, f32[8,128]{1,0:T(8,128)S(1)}, u32[]{:S(2)}, u32[]{:S(2)}) collective-permute-start(f32[8,128]{1,0:T(8,128)S(1)} %get-tuple-element.8), channel_id=1, source_target_pairs={{0,264},{2,266},{4,268},{6,270},{8,256},{10,258},{12,260},{14,262}... | collective-permute-start | bytes 12296 | tf_op jit(solution)/shard_map/ppermute | solution.py:351
  78.8 14.1 %all-gather = bf16[2048,128]{1,0:T(8,128)(2,1)S(1)} all-gather(bf16[256,128]{1,0:T(8,128)(2,1)S(1)} %get-tuple-element.9), channel_id=2, replica_groups=mesh['zh'=2,'y'=4,'x'=4,'zl'=8,'c'=2] {'x','c'}, dimensions={0}, use_global_device_ids=true | all-gather | bytes 589824 | tf_op jit(solution)/shard_map/all_gather | solution.py:352
  92.9 0.6 broadcast_in_dim.2
  93.5 4.9 %all-to-all-start.1 = ((f32[4,8,128]{2,1,0:T(8,128)}), f32[4,8,128]{2,1,0:T(8,128)S(1)}, u32[]{:S(2)}, u32[]{:S(2)}) async-start(f32[4,8,128]{2,1,0:T(8,128)} %broadcast_in_dim.2), calls=%async_computation.1 | async-start | bytes 32768 | tf_op jit(solution)/shard_map/all_to_all | solution.py:354
  98.4 1.3 copy-done.1
  99.7 2.7 %low_conv.1.rows_ref = bf16[64,4,128]{2,1,0:T(4,128)(2,1)S(1)} custom-call(s32[3]{0:T(128)S(1)} %pad_add_fusion.place_ref, bf16[8,256,128]{2,1,0:T(8,128)(2,1)S(1)} %bitcast.36, bf16[8,512,256]{2,1,0:T(8,128)(2,1)S(1)} %all-to-all-done.parts_ref, bf16[8,288,256]{2,1,0:T(8,128)(2,1)S(1)} %copy-done.1), custom_call_target="tpu_custom_call" | custom-call | tf_op jit(solution)/shard_map/low_conv/pallas_call | solution.py:358
  102.4 0.3 all-to-all-done.1.terms_ref
  102.7 24.4 %all_to_all.15 = bf16[192,2,128]{2,1,0:T(2,128)(2,1)S(1)} all-to-all(bf16[192,2,128]{2,1,0:T(2,128)(2,1)S(1)} %bitcast.39), channel_id=1, replica_groups=mesh['zh'=2,'y'=4,'x'=4,'zl'=8,'c'=2] {'x','zl','c'}, dimensions={0} | all-to-all | bytes 196608 | tf_op jit(solution)/shard_map/all_to_all | solution.py:377
  127.1 1.3 join.1
  (26 shorter events, 0.4 us)
Async XLA Ops:
  7.2 29.9 %copy-start.2 = (bf16[1,16,2,8,256]{4,3,2,1,0:T(8,128)(2,1)S(1)}, bf16[1,16,2,8,256]{4,3,2,1,0:T(8,128)(2,1)}, u32[]{:S(2)}) copy-start(bf16[1,16,2,8,256]{4,3,2,1,0:T(8,128)(2,1)} %param.5) | copy-start | bytes 393220
  9.2 37.2 %collective-permute-start.2 = (bf16[504,256]{1,0:T(8,128)(2,1)S(1)}, bf16[504,256]{1,0:T(8,128)(2,1)S(1)}, u32[]{:S(2)}, u32[]{:S(2)}) collective-permute-start(bf16[504,256]{1,0:T(8,128)(2,1)S(1)} %pad_maximum_fusion.1), channel_id=1, source_target_pairs={{8,0},{265,1},{10,2},{267,3},{12,4},{269,5},{14,6},{271,7},{256,8}... | collective-permute-start | bytes 774152 | tf_op jit(solution)/shard_map/ppermute | solution.py:319
  18.9 27.5 %collective-permute-start.1 = (bf16[504,256]{1,0:T(8,128)(2,1)S(1)}, bf16[504,256]{1,0:T(8,128)(2,1)S(1)}, u32[]{:S(2)}, u32[]{:S(2)}) collective-permute-start(bf16[504,256]{1,0:T(8,128)(2,1)S(1)} %pad_maximum_fusion.1), channel_id=1, source_target_pairs={{0,0},{1,1},{2,2},{3,3},{4,4},{5,5},{6,6},{7,7},{8,8},{9,9},{10,10... | collective-permute-start | bytes 774152 | tf_op jit(solution)/shard_map/ppermute | solution.py:318
  20.5 16.5 %collective-permute-start = (bf16[16,8,256]{2,1,0:T(8,128)(2,1)S(1)}, bf16[16,8,256]{2,1,0:T(8,128)(2,1)S(1)}, u32[]{:S(2)}, u32[]{:S(2)}) collective-permute-start(bf16[16,8,256]{2,1,0:T(8,128)(2,1)S(1)} %fusion), channel_id=1, source_target_pairs={{2,1},{4,3},{6,5},{8,7},{10,9},{12,11},{14,13},{16,15},{18,17},{20... | collective-permute-start | bytes 196616 | tf_op jit(solution)/shard_map/ppermute | solution.py:312
  37.7 1.3 copy-start
  39.1 33.7 %all-to-all-start = ((bf16[8,512,256]{2,1,0:T(8,128)(2,1)}), bf16[8,512,256]{2,1,0:T(8,128)(2,1)S(1)}, u32[]{:S(2)}, u32[]{:S(2)}) async-start(bf16[8,512,256]{2,1,0:T(8,128)(2,1)} %bitcast.35), calls=%async_computation | async-start | bytes 4194304 | tf_op jit(solution)/shard_map/all_to_all | solution.py:331
  46.4 26.3 %copy-start.3 = (f32[512]{0:T(512)S(1)}, f32[512]{0:T(512)}, u32[]{:S(2)}) copy-start(f32[512]{0:T(512)} %param.7) | copy-start | bytes 6148
  46.4 52.0 %all-gather.3.cloned.1.call-start = ((), (), s32[]{:S(2)}) async-start(), calls=%async_computation.3 | async-start | bytes 1474560 | tf_op jit(solution)/shard_map/all_gather | solution.py:335
  76.7 16.2 %collective-permute-start.3 = (f32[8,128]{1,0:T(8,128)S(1)}, f32[8,128]{1,0:T(8,128)S(1)}, u32[]{:S(2)}, u32[]{:S(2)}) collective-permute-start(f32[8,128]{1,0:T(8,128)S(1)} %get-tuple-element.8), channel_id=1, source_target_pairs={{0,264},{2,266},{4,268},{6,270},{8,256},{10,258},{12,260},{14,262}... | collective-permute-start | bytes 12296 | tf_op jit(solution)/shard_map/ppermute | solution.py:351
  93.5 9.1 %all-to-all-start.1 = ((f32[4,8,128]{2,1,0:T(8,128)}), f32[4,8,128]{2,1,0:T(8,128)S(1)}, u32[]{:S(2)}, u32[]{:S(2)}) async-start(f32[4,8,128]{2,1,0:T(8,128)} %broadcast_in_dim.2), calls=%async_computation.1 | async-start | bytes 32768 | tf_op jit(solution)/shard_map/all_to_all | solution.py:354
  98.4 1.3 copy-start.1
Sparse Core Ops, SparseCore 0:
  49.3 28.9 all-gather.2

commit v3 on v2

--- a/solution.py
+++ b/solution.py
@@ -49,9 +49,9 @@
     return pltpu.roll(value, 64, 1)
 
 
-def full_mid(parts_ref, source):
+def full_mid(edges_ref, source):
     return jnp.concatenate(
-        [parts_ref[source, 384:448, :], parts_ref[source, 448:512, :]], axis=1
+        [edges_ref[source, 128:192, :], edges_ref[source, 192:256, :]], axis=1
     )
 
 
@@ -59,25 +59,7 @@
     return lax.rsqrt(jnp.mean(mid * mid, axis=1, keepdims=True) + EPSILON)
 
 
-def pack_body(place_ref, rows_ref, halo_ref, mid_ref, out_ref):
-    c = place_ref[1]
-    for core in range(2):
-
-        @pl.when(c == core)
-        def _():
-            for n in range(8):
-                if core == 0:
-                    block = (halo_ref[...], rows_ref[:, 0], rows_ref[:, 1])
-                else:
-                    block = (rows_ref[:, 0], rows_ref[:, 1], halo_ref[...])
-                for r in range(3):
-                    out_ref[n, r] = block[r]
-
-    for n in range(8):
-        out_ref[n, 3] = mid_ref[...]
-
-
-def high_kernel_body(place_ref, parts_ref, weight_ref, gain_ref, out_ref, gain_out_ref, taps_ref, wide_ref):
+def high_kernel_body(place_ref, parts_ref, edges_ref, weight_ref, gain_ref, out_ref, gain_out_ref, taps_ref, wide_ref):
     x, c, z = place_ref[0], place_ref[1], place_ref[2]
     for dy in range(3):
         for dw in range(3):
@@ -94,7 +76,13 @@
     low_half = iota((128, 128), 1) < 64
     for pair in range(4):
         rows = jnp.concatenate(
-            [parts_ref[2 * pair, 0:384, :], parts_ref[2 * pair + 1, 0:384, :]], axis=0
+            [
+                edges_ref[2 * pair, 0:128, :],
+                parts_ref[2 * pair],
+                parts_ref[2 * pair + 1],
+                edges_ref[2 * pair + 1, 0:128, :],
+            ],
+            axis=0,
         )
         product = sum(
             lax.dot_general(
@@ -127,7 +115,7 @@
     half = iota((512, 128), 1) >> 6
     picks = [jnp.where(hit & (half == y), 1.0, 0.0).astype(BF16) for y in range(2)]
     mids = [
-        jnp.concatenate([full_mid(parts_ref, 2 * pair + y) for pair in range(4)], axis=0)
+        jnp.concatenate([full_mid(edges_ref, 2 * pair + y) for pair in range(4)], axis=0)
         for y in range(2)
     ]
     mid = sum(
@@ -160,7 +148,7 @@
     gain_out_ref[...] = terms
 
 
-def low_kernel_body(place_ref, grads_ref, parts_ref, weight_ref, out_ref, turned_ref):
+def low_kernel_body(place_ref, grads_ref, edges_ref, weight_ref, out_ref, turned_ref):
     c, z = place_ref[1], place_ref[2]
     source = iota((256, 256), 0)
     target = (
@@ -182,7 +170,7 @@
     for y in range(2):
         grad = jnp.concatenate([p[:, 128 * y : 128 * y + 128] for p in placed], axis=1)
         mid = jnp.concatenate(
-            [full_mid(parts_ref, 2 * pair + y) for pair in range(4)], axis=0
+            [full_mid(edges_ref, 2 * pair + y) for pair in range(4)], axis=0
         ).astype(F32)
         rms = inverse_rms(mid)
         scaled = mid * rms
@@ -318,17 +306,15 @@
     near = lax.ppermute(kernels, ring, ring_pairs(NEAR))
     far = lax.ppermute(kernels, ring, ring_pairs(FAR))
 
+    def spread(block):
+        return lax.all_to_all(
+            jnp.broadcast_to(block[None], (8, 256, 256)), group, split_axis=0, concat_axis=0, tiled=True
+        )
+
+    parts = spread(jnp.transpose(grad, (1, 0, 2, 3)).reshape(256, 256))
     mid = saved_mid.reshape(64, 512)
-    mid = jnp.concatenate([mid[:, 0:256], mid[:, 256:512]], axis=0).reshape(16, 8, 256)
-    packed = pl.pallas_call(
-        pack_body,
-        out_shape=jax.ShapeDtypeStruct((8, 4, 16, 8, 256), BF16),
-        in_specs=[scalars()] + [whole()] * 3,
-        out_specs=whole(),
-        compiler_params=PARAMS,
-        name="pack_rows",
-    )(place, grad, halo, mid)
-    parts = lax.all_to_all(packed.reshape(8, 512, 256), group, split_axis=0, concat_axis=0, tiled=True)
+    near, far, parts, halo = lax.optimization_barrier((near, far, parts, halo))
+    edges = spread(jnp.concatenate([halo.reshape(128, 256), mid[:, 0:256], mid[:, 256:512]], axis=0))
     high = jnp.concatenate([near[:216].reshape(27, 8, 256), far[:216].reshape(27, 8, 256)], axis=1)
     high_all = lax.all_gather(high.reshape(432, 256), "y", axis=0)
     low = jnp.stack([near[216:], far[216:]], axis=0)
@@ -340,12 +326,12 @@
             jax.ShapeDtypeStruct((256, 128), BF16),
             jax.ShapeDtypeStruct((8, 128), F32),
         ),
-        in_specs=[scalars(), whole(), whole(), whole()],
+        in_specs=[scalars()] + [whole()] * 4,
         out_specs=(whole(), whole()),
         scratch_shapes=[pltpu.VMEM((3, 768, 256), BF16), pltpu.VMEM((512, 128), F32)],
         compiler_params=PARAMS,
         name="high_conv",
-    )(place, parts, high_all, norm_gain.reshape(1, 512))
+    )(place, parts, edges, high_all, norm_gain.reshape(1, 512))
 
     halves = [(z, (z + 4) % 16 if z % 8 >= 4 else (z - 4) % 16) for z in range(16)]
     other = lax.ppermute(gain_terms, ("zh", "zl"), halves)
@@ -363,7 +349,7 @@
         scratch_shapes=[pltpu.VMEM((64, 4, 128), F32)],
         compiler_params=PARAMS,
         name="low_conv",
-    )(place, gathered, parts, low_all)
+    )(place, gathered, edges, low_all)
 
     outgoing = pl.pallas_call(
         close_body,

time: 136 us -> 133 us (0.978)
  waiting for transfers between devices: 21.4 us -> 11.3 us
  starting transfers between devices: 31.8 us -> 37 us
  blocking collectives: 51.3 us -> 55.4 us
    all_to_all x1 -> x2, waiting for transfers between devices: 12.7 us -> 0.01 us  [spread(): lax.all_to_all(jnp.broadcast_to(block[None], (8, 256, 256)), group, split...]
    all_to_all x1 -> x2, starting transfers between devices: 7.32 us -> 17.8 us  [spread(): lax.all_to_all(jnp.broadcast_to(block[None], (8, 256, 256)), group, split...]
    ppermute x1, starting transfers between devices: 9.65 us -> 4.28 us  [shards(): far = lax.ppermute(kernels, ring, ring_pairs(FAR))]
    ppermute x1, waiting for transfers between devices: 8.41 us -> 11.1 us  [shards(): halo = lax.ppermute(edge, shard, halo_pairs)]
    all_gather x1, blocking collectives: 12.7 us -> 15.2 us  [shards(): high_all = lax.all_gather(high.reshape(432, 256), 'y', axis=0)]
    broadcast_in_dim x0 -> x2, local copies, waits for them, and re-layouts: none -> 2.1 us  [spread(): jnp.broadcast_to(block[None], (8, 256, 256))]
    all_gather x1, blocking collectives: 14.1 us -> 16.1 us  [shards(): gathered = lax.all_gather(grads, group, axis=0)]
    unnamed x9 -> x11, local copies, waits for them, and re-layouts: 3.53 us -> 2.2 us
  transfers between devices with their start and end apart: 7 -> 8, of which waited for: 3 -> 2; matrix products, arithmetic and copies ran while one was open for 2% -> 2% of each run, Pallas kernels for 5% -> 5%
where the time goes in v3:
time: 133 us; the launch traced here: 132 us
  blocking collectives  55.4 us (42%)
  starting transfers between devices  37 us (28%)
  between operations  14.2 us (11%)
  waiting for transfers between devices  11.3 us (8%)
  Pallas kernels  8.03 us (6%)
  local copies, waits for them, and re-layouts  5.2 us (4%)
    all_to_all x1, blocking collectives, shards(): lax.all_to_all(outgoing, shard, split_axis=0, concat_axis=0, tiled=True)  24.1 us
    all_to_all x2, starting transfers between devices, spread(): lax.all_to_all(jnp.broadcast_to(block[None], (8, 256, 256)), group, split...  17.8 us
    all_gather x1, blocking collectives, shards(): gathered = lax.all_gather(grads, group, axis=0)  16.1 us
    all_gather x1, blocking collectives, shards(): high_all = lax.all_gather(high.reshape(432, 256), 'y', axis=0)  15.2 us
    ppermute x1, waiting for transfers between devices, shards(): halo = lax.ppermute(edge, shard, halo_pairs)  11.1 us
    ppermute x1, starting transfers between devices, shards(): halo = lax.ppermute(edge, shard, halo_pairs)  6.5 us
    all_to_all x1, starting transfers between devices, shards(): lax.all_to_all(jnp.broadcast_to((gain_terms + other)[None], (4, 8, 128)),...  4.51 us
    ppermute x1, starting transfers between devices, shards(): far = lax.ppermute(kernels, ring, ring_pairs(FAR))  4.28 us
  transfers between devices with their start and end apart: 8, of which 2 were waited for; matrix products, arithmetic and copies ran while one was open for 2% of the time, Pallas kernels for 5%

profile of v3, /device:TPU:1, one launch (start us, length us, event | category | flops | bytes accessed | tf_op | source)
XLA Modules:
  0.0 132.1 jit_solution(4327148508231996620)
XLA Ops:
  7.2 0.9 copy.16
  8.1 1.1 broadcast_in_dim.9
  9.2 10.5 %all-to-all-start = ((bf16[8,256,256]{2,1,0:T(8,128)(2,1)}), bf16[8,256,256]{2,1,0:T(8,128)(2,1)S(1)}, u32[]{:S(2)}, u32[]{:S(2)}) async-start(bf16[8,256,256]{2,1,0:T(8,128)(2,1)} %broadcast_in_dim.9), calls=%async_computation | async-start | bytes 2097152 | tf_op jit(solution)/shard_map/all_to_all | solution.py:310
  19.7 0.1 pad.4
  19.9 0.7 collective-permute-start
  20.6 4.3 %collective-permute-start.1 = (bf16[504,256]{1,0:T(8,128)(2,1)S(1)}, bf16[504,256]{1,0:T(8,128)(2,1)S(1)}, u32[]{:S(2)}, u32[]{:S(2)}) collective-permute-start(bf16[504,256]{1,0:T(8,128)(2,1)S(1)} %pad_maximum_fusion.1), channel_id=1, source_target_pairs={{8,0},{265,1},{10,2},{267,3},{12,4},{269,5},{14,6},{271,7},{256,8}... | collective-permute-start | bytes 774152 | tf_op jit(solution)/shard_map/ppermute | solution.py:307
  24.9 6.5 %collective-permute-start.2 = (bf16[16,8,256]{2,1,0:T(8,128)(2,1)S(1)}, bf16[16,8,256]{2,1,0:T(8,128)(2,1)S(1)}, u32[]{:S(2)}, u32[]{:S(2)}) collective-permute-start(bf16[16,8,256]{2,1,0:T(8,128)(2,1)S(1)} %fusion), channel_id=1, source_target_pairs={{2,1},{4,3},{6,5},{8,7},{10,9},{12,11},{14,13},{16,15},{18,17},{20... | collective-permute-start | bytes 196616 | tf_op jit(solution)/shard_map/ppermute | solution.py:300
  31.4 11.1 %collective-permute-done.2 = bf16[16,8,256]{2,1,0:T(8,128)(2,1)S(1)} collective-permute-done((bf16[16,8,256]{2,1,0:T(8,128)(2,1)S(1)}, bf16[16,8,256]{2,1,0:T(8,128)(2,1)S(1)}, u32[]{:S(2)}, u32[]{:S(2)}) %collective-permute-start.2) | collective-permute-done | bytes 65568 | tf_op jit(solution)/shard_map/ppermute | solution.py:300
  42.5 0.8 pad_maximum_fusion
  43.4 1.0 broadcast_in_dim.10
  44.4 7.4 %all-to-all-start.1 = ((bf16[8,256,256]{2,1,0:T(8,128)(2,1)}), bf16[8,256,256]{2,1,0:T(8,128)(2,1)S(1)}, u32[]{:S(2)}, u32[]{:S(2)}) async-start(bf16[8,256,256]{2,1,0:T(8,128)(2,1)} %broadcast_in_dim.10), calls=%async_computation.1 | async-start | bytes 2097152 | tf_op jit(solution)/shard_map/all_to_all | solution.py:310
  51.8 0.1 pad_add_fusion.place_ref
  51.9 15.2 %all_gather.12.weight_ref = bf16[4,432,256]{2,1,0:T(8,128)(2,1)S(1)} all-gather(bf16[1,432,256]{2,1,0:T(8,128)(2,1)S(1)} %bitcast.42), channel_id=1, replica_groups=mesh['zh'=2,'y'=4,'x'=4,'zl'=8,'c'=2] {'y'}, dimensions={0}, use_global_device_ids=true | all-gather | bytes 1105920 | tf_op jit(solution)/shard_map/all_gather | solution.py:319
  67.2 3.9 %high_conv.1 = (bf16[256,128]{1,0:T(8,128)(2,1)S(1)}, f32[8,128]{1,0:T(8,128)S(1)}) custom-call(s32[3]{0:T(128)S(1)} %pad_add_fusion.place_ref, bf16[8,256,256]{2,1,0:T(8,128)(2,1)S(1)} %all-to-all-done.parts_ref, bf16[8,256,256]{2,1,0:T(8,128)(2,1)S(1)} %all-to-all-done.1.edges_ref, bf16[4,432,256]{2,1,0:T(8,128)(2,1)S(1)} %all_gather.12.weight_ref, ...), custom_call_target="tpu_custom_call" | custom-call | tf_op jit(solution)/shard_map/high_conv/pallas_call | solution.py:323
  71.1 3.2 %collective-permute-start.3 = (f32[8,128]{1,0:T(8,128)S(1)}, f32[8,128]{1,0:T(8,128)S(1)}, u32[]{:S(2)}, u32[]{:S(2)}) collective-permute-start(f32[8,128]{1,0:T(8,128)S(1)} %get-tuple-element.16), channel_id=1, source_target_pairs={{0,264},{2,266},{4,268},{6,270},{8,256},{10,258},{12,260},{14,262}... | collective-permute-start | bytes 12296 | tf_op jit(solution)/shard_map/ppermute | solution.py:337
  74.3 16.1 %all-gather = bf16[2048,128]{1,0:T(8,128)(2,1)S(1)} all-gather(bf16[256,128]{1,0:T(8,128)(2,1)S(1)} %get-tuple-element.17), channel_id=2, replica_groups=mesh['zh'=2,'y'=4,'x'=4,'zl'=8,'c'=2] {'x','c'}, dimensions={0}, use_global_device_ids=true | all-gather | bytes 589824 | tf_op jit(solution)/shard_map/all_gather | solution.py:338
  90.4 0.6 broadcast_in_dim.22
  91.0 4.5 %all-to-all-start.2 = ((f32[4,8,128]{2,1,0:T(8,128)}), f32[4,8,128]{2,1,0:T(8,128)S(1)}, u32[]{:S(2)}, u32[]{:S(2)}) async-start(f32[4,8,128]{2,1,0:T(8,128)} %broadcast_in_dim.22), calls=%async_computation.2 | async-start | bytes 32768 | tf_op jit(solution)/shard_map/all_to_all | solution.py:340
  95.5 1.3 copy-done
  96.8 2.7 %low_conv.1.rows_ref = bf16[64,4,128]{2,1,0:T(4,128)(2,1)S(1)} custom-call(s32[3]{0:T(128)S(1)} %pad_add_fusion.place_ref, bf16[8,256,128]{2,1,0:T(8,128)(2,1)S(1)} %bitcast.36, bf16[8,256,256]{2,1,0:T(8,128)(2,1)S(1)} %all-to-all-done.1.edges_ref, bf16[8,288,256]{2,1,0:T(8,128)(2,1)S(1)} %copy-done), custom_call_target="tpu_custom_call" | custom-call | tf_op jit(solution)/shard_map/low_conv/pallas_call | solution.py:344
  99.5 0.2 all-to-all-done.2.terms_ref
  99.7 0.1 close.1
  99.8 24.1 %all_to_all.20 = bf16[192,2,128]{2,1,0:T(2,128)(2,1)S(1)} all-to-all(bf16[192,2,128]{2,1,0:T(2,128)(2,1)S(1)} %bitcast.38), channel_id=1, replica_groups=mesh['zh'=2,'y'=4,'x'=4,'zl'=8,'c'=2] {'x','zl','c'}, dimensions={0} | all-to-all | bytes 196608 | tf_op jit(solution)/shard_map/all_to_all | solution.py:363
  123.9 1.3 join.1
  (29 shorter events, 0.3 us)
Async XLA Ops:
  9.1 10.5 %copy-start.2 = (bf16[4,27,512]{2,0,1:T(4,128)(2,1)S(1)}, bf16[4,27,512]{2,0,1:T(4,128)(2,1)}, u32[]{:S(2)}) copy-start(bf16[4,27,512]{2,0,1:T(4,128)(2,1)} %param.9) | copy-start | bytes 331780
  9.2 10.7 %copy-start.3 = (bf16[8,27,256]{2,0,1:T(8,128)(2,1)S(1)}, bf16[8,27,256]{2,0,1:T(8,128)(2,1)}, u32[]{:S(2)}) copy-start(bf16[8,27,256]{2,0,1:T(8,128)(2,1)} %param.8) | copy-start | bytes 331780
  9.2 33.3 %all-to-all-start = ((bf16[8,256,256]{2,1,0:T(8,128)(2,1)}), bf16[8,256,256]{2,1,0:T(8,128)(2,1)S(1)}, u32[]{:S(2)}, u32[]{:S(2)}) async-start(bf16[8,256,256]{2,1,0:T(8,128)(2,1)} %broadcast_in_dim.9), calls=%async_computation | async-start | bytes 2097152 | tf_op jit(solution)/shard_map/all_to_all | solution.py:310
  19.6 75.9 %all-gather.3.cloned.1.call-start = ((), (), s32[]{:S(2)}) async-start(), calls=%async_computation.4 | async-start | bytes 1474560 | tf_op jit(solution)/shard_map/all_gather | solution.py:321
  19.8 23.5 %copy-start.4 = (bf16[1,16,1,4,512]{4,3,2,1,0:T(4,128)(2,1)S(1)}, bf16[1,16,1,4,512]{4,3,2,1,0:T(4,128)(2,1)}, u32[]{:S(2)}) copy-start(bf16[1,16,1,4,512]{4,3,2,1,0:T(4,128)(2,1)} %param.6) | copy-start | bytes 196612
  19.9 22.6 %collective-permute-start = (bf16[504,256]{1,0:T(8,128)(2,1)S(1)}, bf16[504,256]{1,0:T(8,128)(2,1)S(1)}, u32[]{:S(2)}, u32[]{:S(2)}) collective-permute-start(bf16[504,256]{1,0:T(8,128)(2,1)S(1)} %pad_maximum_fusion.1), channel_id=1, source_target_pairs={{0,0},{1,1},{2,2},{3,3},{4,4},{5,5},{6,6},{7,7},{8,8},{9,9},{10,10... | collective-permute-start | bytes 774152 | tf_op jit(solution)/shard_map/ppermute | solution.py:306
  20.6 21.9 %collective-permute-start.1 = (bf16[504,256]{1,0:T(8,128)(2,1)S(1)}, bf16[504,256]{1,0:T(8,128)(2,1)S(1)}, u32[]{:S(2)}, u32[]{:S(2)}) collective-permute-start(bf16[504,256]{1,0:T(8,128)(2,1)S(1)} %pad_maximum_fusion.1), channel_id=1, source_target_pairs={{8,0},{265,1},{10,2},{267,3},{12,4},{269,5},{14,6},{271,7},{256,8}... | collective-permute-start | bytes 774152 | tf_op jit(solution)/shard_map/ppermute | solution.py:307
  24.9 17.6 %collective-permute-start.2 = (bf16[16,8,256]{2,1,0:T(8,128)(2,1)S(1)}, bf16[16,8,256]{2,1,0:T(8,128)(2,1)S(1)}, u32[]{:S(2)}, u32[]{:S(2)}) collective-permute-start(bf16[16,8,256]{2,1,0:T(8,128)(2,1)S(1)} %fusion), channel_id=1, source_target_pairs={{2,1},{4,3},{6,5},{8,7},{10,9},{12,11},{14,13},{16,15},{18,17},{20... | collective-permute-start | bytes 196616 | tf_op jit(solution)/shard_map/ppermute | solution.py:300
  44.4 22.8 %all-to-all-start.1 = ((bf16[8,256,256]{2,1,0:T(8,128)(2,1)}), bf16[8,256,256]{2,1,0:T(8,128)(2,1)S(1)}, u32[]{:S(2)}, u32[]{:S(2)}) async-start(bf16[8,256,256]{2,1,0:T(8,128)(2,1)} %broadcast_in_dim.10), calls=%async_computation.1 | async-start | bytes 2097152 | tf_op jit(solution)/shard_map/all_to_all | solution.py:310
  51.8 15.4 %copy-start.1 = (f32[512]{0:T(512)S(1)}, f32[512]{0:T(512)}, u32[]{:S(2)}) copy-start(f32[512]{0:T(512)} %param.7) | copy-start | bytes 6148
  71.1 19.2 %collective-permute-start.3 = (f32[8,128]{1,0:T(8,128)S(1)}, f32[8,128]{1,0:T(8,128)S(1)}, u32[]{:S(2)}, u32[]{:S(2)}) collective-permute-start(f32[8,128]{1,0:T(8,128)S(1)} %get-tuple-element.16), channel_id=1, source_target_pairs={{0,264},{2,266},{4,268},{6,270},{8,256},{10,258},{12,260},{14,262}... | collective-permute-start | bytes 12296 | tf_op jit(solution)/shard_map/ppermute | solution.py:337
  91.0 8.7 %all-to-all-start.2 = ((f32[4,8,128]{2,1,0:T(8,128)}), f32[4,8,128]{2,1,0:T(8,128)S(1)}, u32[]{:S(2)}, u32[]{:S(2)}) async-start(f32[4,8,128]{2,1,0:T(8,128)} %broadcast_in_dim.22), calls=%async_computation.2 | async-start | bytes 32768 | tf_op jit(solution)/shard_map/all_to_all | solution.py:340
  95.5 1.3 copy-start
Sparse Core Ops, SparseCore 0:
  43.4 31.5 all-gather.2

commit v4 on v3

--- a/solution.py
+++ b/solution.py
@@ -148,7 +148,16 @@
     gain_out_ref[...] = terms
 
 
-def low_kernel_body(place_ref, grads_ref, edges_ref, weight_ref, out_ref, turned_ref):
+def low_kernel_body(
+    place_ref, grads_ref, edges_ref, weight_ref, out_ref, turned_ref, taps_ref
+):
+    to, at = iota((144, 112), 0), iota((144, 112), 1)
+    tap = 9 * (to // 48) + 3 * ((to >> 2) & 3) + (to >> 4) % 3
+    pick = jnp.where((at == 4 * tap + (to & 3)) & (((to >> 2) & 3) < 3), 1.0, 0.0).astype(BF16)
+    for n in range(8):
+        taps_ref[n] = jnp.dot(
+            pick, weight_ref[n, 0:112, :], preferred_element_type=F32
+        ).astype(BF16)
     c, z = place_ref[1], place_ref[2]
     source = iota((256, 256), 0)
     target = (
@@ -181,20 +190,10 @@
     frame = (row >> 2) & 15
     column = row & 3
     total = jnp.zeros((512, 128), F32)
-    slots = [slot_of(n, z, c) for n in range(8)]
     for a in range(3):
         for b in range(3):
             at = 16 * (3 * a + b)
-            taps = jnp.concatenate(
-                [
-                    jnp.concatenate(
-                        [weight_ref[n, at : at + 16, :], weight_ref[n, 144 + at : 160 + at, :]],
-                        axis=1,
-                    )
-                    for n in slots
-                ],
-                axis=0,
-            )
+            taps = jnp.concatenate([taps_ref[n, at : at + 16, :] for n in range(8)], axis=0)
             product = lax.dot_general(grads, taps, NT, preferred_element_type=F32)
             moved = row_shift(product, 4 * (2 - a) + 1 - b)
             keep = (frame + 2 - a < 16) & (column + 1 - b >= 0) & (column + 1 - b < 4)
@@ -295,31 +294,28 @@
     shard = ("x", "zl", "c")
 
     grad = grad_out[0]
-    edge = jnp.where(c == 0, grad[:, 0], grad[:, 1])
+    own = jnp.transpose(grad, (1, 0, 2, 3)).reshape(256, 256)
     halo_pairs = [(s, s - 1) for s in range(2, 64, 2)] + [(s, s + 1) for s in range(1, 62, 2)]
-    halo = lax.ppermute(edge, shard, halo_pairs)
-
-    high = jnp.transpose(high_kernel, (1, 0, 2)).reshape(216, 256)
-    low = jnp.transpose(low_kernel.reshape(4, 3, 3, 3, 2, 256), (4, 1, 3, 2, 0, 5))
-    low = jnp.pad(low, ((0, 0), (0, 0), (0, 0), (0, 1), (0, 0), (0, 0))).reshape(288, 256)
-    kernels = jnp.concatenate([high, low], axis=0)
-    near = lax.ppermute(kernels, ring, ring_pairs(NEAR))
-    far = lax.ppermute(kernels, ring, ring_pairs(FAR))
+    halo = lax.ppermute(own, shard, halo_pairs)
+
+    high = jnp.transpose(high_kernel, (1, 0, 2))
+    near = lax.ppermute(high, ring, ring_pairs(NEAR))
+    far = lax.ppermute(high, ring, ring_pairs(FAR))
+    low = jnp.pad(jnp.transpose(low_kernel, (1, 0, 2)).reshape(108, 512), ((0, 20), (0, 0)))
+    low_all = lax.all_gather(low, "zl", axis=0)
 
     def spread(block):
         return lax.all_to_all(
             jnp.broadcast_to(block[None], (8, 256, 256)), group, split_axis=0, concat_axis=0, tiled=True
         )
 
-    parts = spread(jnp.transpose(grad, (1, 0, 2, 3)).reshape(256, 256))
+    parts = spread(own)
     mid = saved_mid.reshape(64, 512)
-    near, far, parts, halo = lax.optimization_barrier((near, far, parts, halo))
-    edges = spread(jnp.concatenate([halo.reshape(128, 256), mid[:, 0:256], mid[:, 256:512]], axis=0))
-    high = jnp.concatenate([near[:216].reshape(27, 8, 256), far[:216].reshape(27, 8, 256)], axis=1)
+    halo, parts, near, far = lax.optimization_barrier((halo, parts, near, far))
+    halo = jnp.where(c == 0, halo[128:256], halo[0:128])
+    edges = spread(jnp.concatenate([halo, mid[:, 0:256], mid[:, 256:512]], axis=0))
+    high = jnp.concatenate([near, far], axis=1)
     high_all = lax.all_gather(high.reshape(432, 256), "y", axis=0)
-    low = jnp.stack([near[216:], far[216:]], axis=0)
-    low_all = lax.all_gather(low, "y", axis=0, tiled=True)
-
     grads, gain_terms = pl.pallas_call(
         high_kernel_body,
         out_shape=(
@@ -346,7 +342,7 @@
         out_shape=jax.ShapeDtypeStruct((64, 4, 128), BF16),
         in_specs=[scalars(), whole(), whole(), whole()],
         out_specs=whole(),
-        scratch_shapes=[pltpu.VMEM((64, 4, 128), F32)],
+        scratch_shapes=[pltpu.VMEM((64, 4, 128), F32), pltpu.VMEM((8, 144, 512), BF16)],
         compiler_params=PARAMS,
         name="low_conv",
     )(place, gathered, edges, low_all)

time: 133 us -> 125 us (0.940)
  waiting for transfers between devices: 11.3 us -> 5.88 us
  blocking collectives: 55.4 us -> 52.2 us
    ppermute x3, waiting for transfers between devices: 11.1 us -> 5.14 us  [the longest x1 5.13 us: shards(): far = lax.ppermute(high, ring, ring_pairs(FAR))]
    ppermute x3, starting transfers between devices: 11.5 us -> 8.43 us  [the longest x1 5.84 us: shards(): far = lax.ppermute(high, ring, ring_pairs(FAR))]
    all_to_all x2, starting transfers between devices: 17.8 us -> 20.5 us  [spread(): lax.all_to_all(jnp.broadcast_to(block[None], (8, 256, 256)), group, split...]
    all_to_all x1, blocking collectives: 24.1 us -> 21.7 us  [shards(): lax.all_to_all(outgoing, shard, split_axis=0, concat_axis=0, tiled=True)]
    all_gather x1, blocking collectives: 16.1 us -> 14.1 us  [shards(): gathered = lax.all_gather(grads, group, axis=0)]
    ppermute x1, starting transfers between devices: 3.15 us -> 5.03 us  [shards(): other = lax.ppermute(gain_terms, ('zh', 'zl'), halves)]
  transfers between devices with their start and end apart: 8 -> 8, of which waited for: 2 -> 2; matrix products, arithmetic and copies ran while one was open for 2% -> 2% of each run, Pallas kernels for 5% -> 6%
where the time goes in v4:
time: 125 us; the launch traced here: 124 us
  blocking collectives  52.2 us (42%)
  starting transfers between devices  38 us (30%)
  between operations  14.2 us (11%)
  Pallas kernels  8.29 us (7%)
  waiting for transfers between devices  5.88 us (5%)
  local copies, waits for them, and re-layouts  5.59 us (4%)
    all_to_all x1, blocking collectives, shards(): lax.all_to_all(outgoing, shard, split_axis=0, concat_axis=0, tiled=True)  21.7 us
    all_to_all x2, starting transfers between devices, spread(): lax.all_to_all(jnp.broadcast_to(block[None], (8, 256, 256)), group, split...  20.5 us
    all_gather x1, blocking collectives, shards(): high_all = lax.all_gather(high.reshape(432, 256), 'y', axis=0)  16.4 us
    all_gather x1, blocking collectives, shards(): gathered = lax.all_gather(grads, group, axis=0)  14.1 us
    ppermute x1, starting transfers between devices, shards(): far = lax.ppermute(high, ring, ring_pairs(FAR))  5.84 us
    ppermute x1, waiting for transfers between devices, shards(): far = lax.ppermute(high, ring, ring_pairs(FAR))  5.13 us
    ppermute x1, starting transfers between devices, shards(): other = lax.ppermute(gain_terms, ('zh', 'zl'), halves)  5.03 us
    all_to_all x1, starting transfers between devices, shards(): lax.all_to_all(jnp.broadcast_to((gain_terms + other)[None], (4, 8, 128)),...  4.02 us
  transfers between devices with their start and end apart: 8, of which 2 were waited for; matrix products, arithmetic and copies ran while one was open for 2% of the time, Pallas kernels for 6%

profile of v4, /device:TPU:1, one launch (start us, length us, event | category | flops | bytes accessed | tf_op | source)
XLA Modules:
  0.0 124.2 jit_solution(2539765154761645380)
XLA Ops:
  7.2 0.9 copy.8
  8.1 1.0 broadcast_in_dim.6
  9.1 10.5 %all-to-all-start = ((bf16[8,256,256]{2,1,0:T(8,128)(2,1)}), bf16[8,256,256]{2,1,0:T(8,128)(2,1)S(1)}, u32[]{:S(2)}, u32[]{:S(2)}) async-start(bf16[8,256,256]{2,1,0:T(8,128)(2,1)} %broadcast_in_dim.6), calls=%async_computation | async-start | bytes 2097152 | tf_op jit(solution)/shard_map/all_to_all | solution.py:308
  19.7 0.7 pad.4
  20.3 0.0 all-gather.4.cloned.1.call-update
  20.3 1.9 %collective-permute-start = (bf16[256,256]{1,0:T(8,128)(2,1)S(1)}, bf16[256,256]{1,0:T(8,128)(2,1)S(1)}, u32[]{:S(2)}, u32[]{:S(2)}) collective-permute-start(bf16[256,256]{1,0:T(8,128)(2,1)S(1)} %bitcast.25), channel_id=1, source_target_pairs={{2,1},{4,3},{6,5},{8,7},{10,9},{12,11},{14,13},{16,15},{18,17},{20... | collective-permute-start | bytes 393224 | tf_op jit(solution)/shard_map/ppermute | solution.py:299
  22.3 0.7 collective-permute-start.1
  23.0 5.8 %collective-permute-start.2 = (bf16[27,8,256]{2,1,0:T(8,128)(2,1)S(1)}, bf16[27,8,256]{2,1,0:T(8,128)(2,1)S(1)}, u32[]{:S(2)}, u32[]{:S(2)}) collective-permute-start(bf16[27,8,256]{2,1,0:T(8,128)(2,1)S(1)} %bitcast.28), channel_id=1, source_target_pairs={{8,0},{265,1},{10,2},{267,3},{12,4},{269,5},{14,6},{271,7},{256,8}... | collective-permute-start | bytes 331784 | tf_op jit(solution)/shard_map/ppermute | solution.py:303
  28.9 5.1 %collective-permute-done.2 = bf16[27,8,256]{2,1,0:T(8,128)(2,1)S(1)} collective-permute-done((bf16[27,8,256]{2,1,0:T(8,128)(2,1)S(1)}, bf16[27,8,256]{2,1,0:T(8,128)(2,1)S(1)}, u32[]{:S(2)}, u32[]{:S(2)}) %collective-permute-start.2) | collective-permute-done | bytes 110624 | tf_op jit(solution)/shard_map/ppermute | solution.py:303
  34.0 0.7 all-to-all-done.parts_ref
  34.8 1.0 broadcast_in_dim.7
  35.8 10.1 %all-to-all-start.1 = ((bf16[8,256,256]{2,1,0:T(8,128)(2,1)}), bf16[8,256,256]{2,1,0:T(8,128)(2,1)S(1)}, u32[]{:S(2)}, u32[]{:S(2)}) async-start(bf16[8,256,256]{2,1,0:T(8,128)(2,1)} %broadcast_in_dim.7), calls=%async_computation.1 | async-start | bytes 2097152 | tf_op jit(solution)/shard_map/all_to_all | solution.py:308
  45.9 0.1 pad_add_fusion.place_ref
  46.0 16.4 %all_gather.15.weight_ref = bf16[4,432,256]{2,1,0:T(8,128)(2,1)S(1)} all-gather(bf16[1,432,256]{2,1,0:T(8,128)(2,1)S(1)} %bitcast.23), channel_id=1, replica_groups=mesh['zh'=2,'y'=4,'x'=4,'zl'=8,'c'=2] {'y'}, dimensions={0}, use_global_device_ids=true | all-gather | bytes 1105920 | tf_op jit(solution)/shard_map/all_gather | solution.py:318
  62.3 3.9 %high_conv.1 = (bf16[256,128]{1,0:T(8,128)(2,1)S(1)}, f32[8,128]{1,0:T(8,128)S(1)}) custom-call(s32[3]{0:T(128)S(1)} %pad_add_fusion.place_ref, bf16[8,256,256]{2,1,0:T(8,128)(2,1)S(1)} %all-to-all-done.parts_ref, bf16[8,256,256]{2,1,0:T(8,128)(2,1)S(1)} %all-to-all-done.1.edges_ref, bf16[4,432,256]{2,1,0:T(8,128)(2,1)S(1)} %all_gather.15.weight_ref, ...), custom_call_target="tpu_custom_call" | custom-call | tf_op jit(solution)/shard_map/high_conv/pallas_call | solution.py:319
  66.3 5.0 %collective-permute-start.3 = (f32[8,128]{1,0:T(8,128)S(1)}, f32[8,128]{1,0:T(8,128)S(1)}, u32[]{:S(2)}, u32[]{:S(2)}) collective-permute-start(f32[8,128]{1,0:T(8,128)S(1)} %get-tuple-element.16), channel_id=1, source_target_pairs={{0,264},{2,266},{4,268},{6,270},{8,256},{10,258},{12,260},{14,262}... | collective-permute-start | bytes 12296 | tf_op jit(solution)/shard_map/ppermute | solution.py:333
  71.3 14.1 %all-gather = bf16[2048,128]{1,0:T(8,128)(2,1)S(1)} all-gather(bf16[256,128]{1,0:T(8,128)(2,1)S(1)} %get-tuple-element.17), channel_id=2, replica_groups=mesh['zh'=2,'y'=4,'x'=4,'zl'=8,'c'=2] {'x','c'}, dimensions={0}, use_global_device_ids=true | all-gather | bytes 589824 | tf_op jit(solution)/shard_map/all_gather | solution.py:334
  85.4 0.6 broadcast_in_dim.8
  86.1 4.0 %all-to-all-start.2 = ((f32[4,8,128]{2,1,0:T(8,128)}), f32[4,8,128]{2,1,0:T(8,128)S(1)}, u32[]{:S(2)}, u32[]{:S(2)}) async-start(f32[4,8,128]{2,1,0:T(8,128)} %broadcast_in_dim.8), calls=%async_computation.2 | async-start | bytes 32768 | tf_op jit(solution)/shard_map/all_to_all | solution.py:336
  90.1 1.2 copy-done
  91.3 3.0 %low_conv.1.rows_ref = bf16[64,4,128]{2,1,0:T(4,128)(2,1)S(1)} custom-call(s32[3]{0:T(128)S(1)} %pad_add_fusion.place_ref, bf16[8,256,128]{2,1,0:T(8,128)(2,1)S(1)} %bitcast.18, bf16[8,256,256]{2,1,0:T(8,128)(2,1)S(1)} %all-to-all-done.1.edges_ref, bf16[8,128,512]{2,1,0:T(8,128)(2,1)S(1)} %bitcast.19), custom_call_target="tpu_custom_call" | custom-call | tf_op jit(solution)/shard_map/low_conv/pallas_call | solution.py:340
  94.3 0.1 close.1
  94.4 21.7 %all_to_all.20 = bf16[192,2,128]{2,1,0:T(2,128)(2,1)S(1)} all-to-all(bf16[192,2,128]{2,1,0:T(2,128)(2,1)S(1)} %bitcast.21), channel_id=1, replica_groups=mesh['zh'=2,'y'=4,'x'=4,'zl'=8,'c'=2] {'x','zl','c'}, dimensions={0} | all-to-all | bytes 196608 | tf_op jit(solution)/shard_map/all_to_all | solution.py:359
  116.1 1.3 %join.1 = (bf16[64,256]{1,0:T(8,128)(2,1)}, f32[4,128]{1,0:T(4,128)}) custom-call(bf16[64,3,2,128]{3,2,1,0:T(2,128)(2,1)S(1)} %bitcast.20), custom_call_target="tpu_custom_call" | custom-call | tf_op jit(solution)/shard_map/join/pallas_call | solution.py:362
  (23 shorter events, 0.1 us)
Async XLA Ops:
  9.1 10.5 %copy-start.2 = (bf16[4,27,512]{2,0,1:T(4,128)(2,1)S(1)}, bf16[4,27,512]{2,0,1:T(4,128)(2,1)}, u32[]{:S(2)}) copy-start(bf16[4,27,512]{2,0,1:T(4,128)(2,1)} %param.9) | copy-start | bytes 331780
  9.1 25.6 %all-to-all-start = ((bf16[8,256,256]{2,1,0:T(8,128)(2,1)}), bf16[8,256,256]{2,1,0:T(8,128)(2,1)S(1)}, u32[]{:S(2)}, u32[]{:S(2)}) async-start(bf16[8,256,256]{2,1,0:T(8,128)(2,1)} %broadcast_in_dim.6), calls=%async_computation | async-start | bytes 2097152 | tf_op jit(solution)/shard_map/all_to_all | solution.py:308
  19.6 70.5 %all-gather.4.cloned.1.call-start = ((), (), s32[]{:S(2)}) async-start(), calls=%async_computation.4 | async-start | bytes 1179648 | tf_op jit(solution)/shard_map/all_gather | solution.py:305
  19.6 2.6 %copy-start.4 = (bf16[8,27,256]{2,0,1:T(8,128)(2,1)S(1)}, bf16[8,27,256]{2,0,1:T(8,128)(2,1)}, u32[]{:S(2)}) copy-start(bf16[8,27,256]{2,0,1:T(8,128)(2,1)} %param.8) | copy-start | bytes 331780
  20.3 8.5 %copy-start.3 = (bf16[1,16,1,4,512]{4,3,2,1,0:T(4,128)(2,1)S(1)}, bf16[1,16,1,4,512]{4,3,2,1,0:T(4,128)(2,1)}, u32[]{:S(2)}) copy-start(bf16[1,16,1,4,512]{4,3,2,1,0:T(4,128)(2,1)} %param.6) | copy-start | bytes 196612
  20.3 13.7 %collective-permute-start = (bf16[256,256]{1,0:T(8,128)(2,1)S(1)}, bf16[256,256]{1,0:T(8,128)(2,1)S(1)}, u32[]{:S(2)}, u32[]{:S(2)}) collective-permute-start(bf16[256,256]{1,0:T(8,128)(2,1)S(1)} %bitcast.25), channel_id=1, source_target_pairs={{2,1},{4,3},{6,5},{8,7},{10,9},{12,11},{14,13},{16,15},{18,17},{20... | collective-permute-start | bytes 393224 | tf_op jit(solution)/shard_map/ppermute | solution.py:299
  22.3 6.6 %collective-permute-start.1 = (bf16[27,8,256]{2,1,0:T(8,128)(2,1)S(1)}, bf16[27,8,256]{2,1,0:T(8,128)(2,1)S(1)}, u32[]{:S(2)}, u32[]{:S(2)}) collective-permute-start(bf16[27,8,256]{2,1,0:T(8,128)(2,1)S(1)} %bitcast.27), channel_id=1, source_target_pairs={{0,0},{1,1},{2,2},{3,3},{4,4},{5,5},{6,6},{7,7},{8,8},{9,9},{10,10... | collective-permute-start | bytes 331784 | tf_op jit(solution)/shard_map/ppermute | solution.py:302
  23.0 11.0 %collective-permute-start.2 = (bf16[27,8,256]{2,1,0:T(8,128)(2,1)S(1)}, bf16[27,8,256]{2,1,0:T(8,128)(2,1)S(1)}, u32[]{:S(2)}, u32[]{:S(2)}) collective-permute-start(bf16[27,8,256]{2,1,0:T(8,128)(2,1)S(1)} %bitcast.28), channel_id=1, source_target_pairs={{8,0},{265,1},{10,2},{267,3},{12,4},{269,5},{14,6},{271,7},{256,8}... | collective-permute-start | bytes 331784 | tf_op jit(solution)/shard_map/ppermute | solution.py:303
  35.8 26.5 %all-to-all-start.1 = ((bf16[8,256,256]{2,1,0:T(8,128)(2,1)}), bf16[8,256,256]{2,1,0:T(8,128)(2,1)S(1)}, u32[]{:S(2)}, u32[]{:S(2)}) async-start(bf16[8,256,256]{2,1,0:T(8,128)(2,1)} %broadcast_in_dim.7), calls=%async_computation.1 | async-start | bytes 2097152 | tf_op jit(solution)/shard_map/all_to_all | solution.py:308
  45.9 16.4 %copy-start.1 = (f32[512]{0:T(512)S(1)}, f32[512]{0:T(512)}, u32[]{:S(2)}) copy-start(f32[512]{0:T(512)} %param.7) | copy-start | bytes 6148
  66.3 19.1 %collective-permute-start.3 = (f32[8,128]{1,0:T(8,128)S(1)}, f32[8,128]{1,0:T(8,128)S(1)}, u32[]{:S(2)}, u32[]{:S(2)}) collective-permute-start(f32[8,128]{1,0:T(8,128)S(1)} %get-tuple-element.16), channel_id=1, source_target_pairs={{0,264},{2,266},{4,268},{6,270},{8,256},{10,258},{12,260},{14,262}... | collective-permute-start | bytes 12296 | tf_op jit(solution)/shard_map/ppermute | solution.py:333
  86.1 8.2 %all-to-all-start.2 = ((f32[4,8,128]{2,1,0:T(8,128)}), f32[4,8,128]{2,1,0:T(8,128)S(1)}, u32[]{:S(2)}, u32[]{:S(2)}) async-start(f32[4,8,128]{2,1,0:T(8,128)} %broadcast_in_dim.8), calls=%async_computation.2 | async-start | bytes 32768 | tf_op jit(solution)/shard_map/all_to_all | solution.py:336
  90.1 1.2 copy-start
Sparse Core Ops, SparseCore 0:
  22.5 60.7 all-gather.3

commit v5 on v4

--- a/solution.py
+++ b/solution.py
@@ -149,7 +149,7 @@
 
 
 def low_kernel_body(
-    place_ref, grads_ref, edges_ref, weight_ref, out_ref, turned_ref, taps_ref
+    place_ref, grads_ref, edges_ref, weight_ref, out_ref, taps_ref
 ):
     to, at = iota((144, 112), 0), iota((144, 112), 1)
     tap = 9 * (to // 48) + 3 * ((to >> 2) & 3) + (to >> 4) % 3
@@ -200,8 +200,7 @@
             total = total + jnp.where(keep, moved, 0.0)
     result = total[0:256] + pltpu.roll(total[256:512], 4, 1)
     for pair in range(4):
-        turned_ref[:, pair, :] = result[64 * pair : 64 * pair + 64]
-    out_ref[...] = turned_ref[...].astype(BF16)
+        out_ref[:, pair, :] = result[64 * pair : 64 * pair + 64]
 
 
 def close_body(rows_ref, terms_ref, out_ref):
@@ -210,8 +209,8 @@
         terms = terms + terms_ref[n]
     head = terms.astype(BF16).astype(F32)
     line = jnp.where(iota((8, 128), 1) < 64, head, terms - head)[0:2].astype(BF16)
-    out_ref[:, 0] = rows_ref[:, 0:2]
-    out_ref[:, 1] = rows_ref[:, 2:4]
+    out_ref[:, 0] = rows_ref[:, 0:2].astype(BF16)
+    out_ref[:, 1] = rows_ref[:, 2:4].astype(BF16)
     out_ref[:, 2] = jnp.broadcast_to(line[None], (64, 2, 128))
 
 
@@ -339,10 +338,10 @@
 
     partial = pl.pallas_call(
         low_kernel_body,
-        out_shape=jax.ShapeDtypeStruct((64, 4, 128), BF16),
+        out_shape=jax.ShapeDtypeStruct((64, 4, 128), F32),
         in_specs=[scalars(), whole(), whole(), whole()],
         out_specs=whole(),
-        scratch_shapes=[pltpu.VMEM((64, 4, 128), F32), pltpu.VMEM((8, 144, 512), BF16)],
+        scratch_shapes=[pltpu.VMEM((8, 144, 512), BF16)],
         compiler_params=PARAMS,
         name="low_conv",
     )(place, gathered, edges, low_all)

time: 125 us -> 125 us (level)
  no operation moved by 1% of the time
where the time goes in v5:
time: 125 us; the launch traced here: 124 us
  blocking collectives  52.2 us (42%)
  starting transfers between devices  38 us (30%)
  between operations  14.2 us (11%)
  Pallas kernels  8.26 us (7%)
  waiting for transfers between devices  5.9 us (5%)
  local copies, waits for them, and re-layouts  5.59 us (4%)
    all_to_all x1, blocking collectives, shards(): lax.all_to_all(outgoing, shard, split_axis=0, concat_axis=0, tiled=True)  21.7 us
    all_to_all x2, starting transfers between devices, spread(): lax.all_to_all(jnp.broadcast_to(block[None], (8, 256, 256)), group, split...  20.5 us
    all_gather x1, blocking collectives, shards(): high_all = lax.all_gather(high.reshape(432, 256), 'y', axis=0)  16.4 us
    all_gather x1, blocking collectives, shards(): gathered = lax.all_gather(grads, group, axis=0)  14.1 us
    ppermute x1, starting transfers between devices, shards(): far = lax.ppermute(high, ring, ring_pairs(FAR))  5.84 us
    ppermute x1, waiting for transfers between devices, shards(): far = lax.ppermute(high, ring, ring_pairs(FAR))  5.13 us
    ppermute x1, starting transfers between devices, shards(): other = lax.ppermute(gain_terms, ('zh', 'zl'), halves)  5.03 us
    all_to_all x1, starting transfers between devices, shards(): lax.all_to_all(jnp.broadcast_to((gain_terms + other)[None], (4, 8, 128)),...  4.02 us
  transfers between devices with their start and end apart: 8, of which 2 were waited for; matrix products, arithmetic and copies ran while one was open for 2% of the time, Pallas kernels for 6%

profile of v5, /device:TPU:1, one launch (start us, length us, event | category | flops | bytes accessed | tf_op | source)
XLA Modules:
  0.0 124.2 jit_solution(5475810307348813042)
XLA Ops:
  7.2 0.9 copy.8
  8.1 1.0 broadcast_in_dim.6
  9.1 10.5 %all-to-all-start = ((bf16[8,256,256]{2,1,0:T(8,128)(2,1)}), bf16[8,256,256]{2,1,0:T(8,128)(2,1)S(1)}, u32[]{:S(2)}, u32[]{:S(2)}) async-start(bf16[8,256,256]{2,1,0:T(8,128)(2,1)} %broadcast_in_dim.6), calls=%async_computation | async-start | bytes 2097152 | tf_op jit(solution)/shard_map/all_to_all | solution.py:307
  19.7 0.7 pad.4
  20.3 1.9 %collective-permute-start = (bf16[256,256]{1,0:T(8,128)(2,1)S(1)}, bf16[256,256]{1,0:T(8,128)(2,1)S(1)}, u32[]{:S(2)}, u32[]{:S(2)}) collective-permute-start(bf16[256,256]{1,0:T(8,128)(2,1)S(1)} %bitcast.25), channel_id=1, source_target_pairs={{2,1},{4,3},{6,5},{8,7},{10,9},{12,11},{14,13},{16,15},{18,17},{20... | collective-permute-start | bytes 393224 | tf_op jit(solution)/shard_map/ppermute | solution.py:298
  22.3 0.7 collective-permute-start.1
  23.0 5.8 %collective-permute-start.2 = (bf16[27,8,256]{2,1,0:T(8,128)(2,1)S(1)}, bf16[27,8,256]{2,1,0:T(8,128)(2,1)S(1)}, u32[]{:S(2)}, u32[]{:S(2)}) collective-permute-start(bf16[27,8,256]{2,1,0:T(8,128)(2,1)S(1)} %bitcast.28), channel_id=1, source_target_pairs={{8,0},{265,1},{10,2},{267,3},{12,4},{269,5},{14,6},{271,7},{256,8}... | collective-permute-start | bytes 331784 | tf_op jit(solution)/shard_map/ppermute | solution.py:302
  28.9 5.1 %collective-permute-done.2 = bf16[27,8,256]{2,1,0:T(8,128)(2,1)S(1)} collective-permute-done((bf16[27,8,256]{2,1,0:T(8,128)(2,1)S(1)}, bf16[27,8,256]{2,1,0:T(8,128)(2,1)S(1)}, u32[]{:S(2)}, u32[]{:S(2)}) %collective-permute-start.2) | collective-permute-done | bytes 110624 | tf_op jit(solution)/shard_map/ppermute | solution.py:302
  34.0 0.7 all-to-all-done.parts_ref
  34.8 1.0 broadcast_in_dim.7
  35.8 10.1 %all-to-all-start.1 = ((bf16[8,256,256]{2,1,0:T(8,128)(2,1)}), bf16[8,256,256]{2,1,0:T(8,128)(2,1)S(1)}, u32[]{:S(2)}, u32[]{:S(2)}) async-start(bf16[8,256,256]{2,1,0:T(8,128)(2,1)} %broadcast_in_dim.7), calls=%async_computation.1 | async-start | bytes 2097152 | tf_op jit(solution)/shard_map/all_to_all | solution.py:307
  45.9 0.1 pad_add_fusion.place_ref
  46.0 16.4 %all_gather.15.weight_ref = bf16[4,432,256]{2,1,0:T(8,128)(2,1)S(1)} all-gather(bf16[1,432,256]{2,1,0:T(8,128)(2,1)S(1)} %bitcast.23), channel_id=1, replica_groups=mesh['zh'=2,'y'=4,'x'=4,'zl'=8,'c'=2] {'y'}, dimensions={0}, use_global_device_ids=true | all-gather | bytes 1105920 | tf_op jit(solution)/shard_map/all_gather | solution.py:317
  62.3 3.9 %high_conv.1 = (bf16[256,128]{1,0:T(8,128)(2,1)S(1)}, f32[8,128]{1,0:T(8,128)S(1)}) custom-call(s32[3]{0:T(128)S(1)} %pad_add_fusion.place_ref, bf16[8,256,256]{2,1,0:T(8,128)(2,1)S(1)} %all-to-all-done.parts_ref, bf16[8,256,256]{2,1,0:T(8,128)(2,1)S(1)} %all-to-all-done.1.edges_ref, bf16[4,432,256]{2,1,0:T(8,128)(2,1)S(1)} %all_gather.15.weight_ref, ...), custom_call_target="tpu_custom_call" | custom-call | tf_op jit(solution)/shard_map/high_conv/pallas_call | solution.py:318
  66.3 5.0 %collective-permute-start.3 = (f32[8,128]{1,0:T(8,128)S(1)}, f32[8,128]{1,0:T(8,128)S(1)}, u32[]{:S(2)}, u32[]{:S(2)}) collective-permute-start(f32[8,128]{1,0:T(8,128)S(1)} %get-tuple-element.16), channel_id=1, source_target_pairs={{0,264},{2,266},{4,268},{6,270},{8,256},{10,258},{12,260},{14,262}... | collective-permute-start | bytes 12296 | tf_op jit(solution)/shard_map/ppermute | solution.py:332
  71.3 14.1 %all-gather = bf16[2048,128]{1,0:T(8,128)(2,1)S(1)} all-gather(bf16[256,128]{1,0:T(8,128)(2,1)S(1)} %get-tuple-element.17), channel_id=2, replica_groups=mesh['zh'=2,'y'=4,'x'=4,'zl'=8,'c'=2] {'x','c'}, dimensions={0}, use_global_device_ids=true | all-gather | bytes 589824 | tf_op jit(solution)/shard_map/all_gather | solution.py:333
  85.4 0.6 broadcast_in_dim.8
  86.1 4.0 %all-to-all-start.2 = ((f32[4,8,128]{2,1,0:T(8,128)}), f32[4,8,128]{2,1,0:T(8,128)S(1)}, u32[]{:S(2)}, u32[]{:S(2)}) async-start(f32[4,8,128]{2,1,0:T(8,128)} %broadcast_in_dim.8), calls=%async_computation.2 | async-start | bytes 32768 | tf_op jit(solution)/shard_map/all_to_all | solution.py:335
  90.1 1.2 copy-done
  91.3 2.9 %low_conv.1.rows_ref = f32[64,4,128]{2,1,0:T(4,128)S(1)} custom-call(s32[3]{0:T(128)S(1)} %pad_add_fusion.place_ref, bf16[8,256,128]{2,1,0:T(8,128)(2,1)S(1)} %bitcast.18, bf16[8,256,256]{2,1,0:T(8,128)(2,1)S(1)} %all-to-all-done.1.edges_ref, bf16[8,128,512]{2,1,0:T(8,128)(2,1)S(1)} %bitcast.19), custom_call_target="tpu_custom_call" | custom-call | tf_op jit(solution)/shard_map/low_conv/pallas_call | solution.py:339
  94.3 0.0 all-to-all-done.2.terms_ref
  94.3 0.1 close.1
  94.4 21.7 %all_to_all.20 = bf16[192,2,128]{2,1,0:T(2,128)(2,1)S(1)} all-to-all(bf16[192,2,128]{2,1,0:T(2,128)(2,1)S(1)} %bitcast.21), channel_id=1, replica_groups=mesh['zh'=2,'y'=4,'x'=4,'zl'=8,'c'=2] {'x','zl','c'}, dimensions={0} | all-to-all | bytes 196608 | tf_op jit(solution)/shard_map/all_to_all | solution.py:358
  116.1 1.3 %join.1 = (bf16[64,256]{1,0:T(8,128)(2,1)}, f32[4,128]{1,0:T(4,128)}) custom-call(bf16[64,3,2,128]{3,2,1,0:T(2,128)(2,1)S(1)} %bitcast.20), custom_call_target="tpu_custom_call" | custom-call | tf_op jit(solution)/shard_map/join/pallas_call | solution.py:361
  (23 shorter events, 0.2 us)
Async XLA Ops:
  9.1 10.5 %copy-start.2 = (bf16[4,27,512]{2,0,1:T(4,128)(2,1)S(1)}, bf16[4,27,512]{2,0,1:T(4,128)(2,1)}, u32[]{:S(2)}) copy-start(bf16[4,27,512]{2,0,1:T(4,128)(2,1)} %param.9) | copy-start | bytes 331780
  9.1 25.6 %all-to-all-start = ((bf16[8,256,256]{2,1,0:T(8,128)(2,1)}), bf16[8,256,256]{2,1,0:T(8,128)(2,1)S(1)}, u32[]{:S(2)}, u32[]{:S(2)}) async-start(bf16[8,256,256]{2,1,0:T(8,128)(2,1)} %broadcast_in_dim.6), calls=%async_computation | async-start | bytes 2097152 | tf_op jit(solution)/shard_map/all_to_all | solution.py:307
  19.6 70.5 %all-gather.4.cloned.1.call-start = ((), (), s32[]{:S(2)}) async-start(), calls=%async_computation.4 | async-start | bytes 1179648 | tf_op jit(solution)/shard_map/all_gather | solution.py:304
  19.6 2.6 %copy-start.4 = (bf16[8,27,256]{2,0,1:T(8,128)(2,1)S(1)}, bf16[8,27,256]{2,0,1:T(8,128)(2,1)}, u32[]{:S(2)}) copy-start(bf16[8,27,256]{2,0,1:T(8,128)(2,1)} %param.8) | copy-start | bytes 331780
  20.3 8.5 %copy-start.3 = (bf16[1,16,1,4,512]{4,3,2,1,0:T(4,128)(2,1)S(1)}, bf16[1,16,1,4,512]{4,3,2,1,0:T(4,128)(2,1)}, u32[]{:S(2)}) copy-start(bf16[1,16,1,4,512]{4,3,2,1,0:T(4,128)(2,1)} %param.6) | copy-start | bytes 196612
  20.3 13.7 %collective-permute-start = (bf16[256,256]{1,0:T(8,128)(2,1)S(1)}, bf16[256,256]{1,0:T(8,128)(2,1)S(1)}, u32[]{:S(2)}, u32[]{:S(2)}) collective-permute-start(bf16[256,256]{1,0:T(8,128)(2,1)S(1)} %bitcast.25), channel_id=1, source_target_pairs={{2,1},{4,3},{6,5},{8,7},{10,9},{12,11},{14,13},{16,15},{18,17},{20... | collective-permute-start | bytes 393224 | tf_op jit(solution)/shard_map/ppermute | solution.py:298
  22.3 6.6 %collective-permute-start.1 = (bf16[27,8,256]{2,1,0:T(8,128)(2,1)S(1)}, bf16[27,8,256]{2,1,0:T(8,128)(2,1)S(1)}, u32[]{:S(2)}, u32[]{:S(2)}) collective-permute-start(bf16[27,8,256]{2,1,0:T(8,128)(2,1)S(1)} %bitcast.27), channel_id=1, source_target_pairs={{0,0},{1,1},{2,2},{3,3},{4,4},{5,5},{6,6},{7,7},{8,8},{9,9},{10,10... | collective-permute-start | bytes 331784 | tf_op jit(solution)/shard_map/ppermute | solution.py:301
  23.0 11.0 %collective-permute-start.2 = (bf16[27,8,256]{2,1,0:T(8,128)(2,1)S(1)}, bf16[27,8,256]{2,1,0:T(8,128)(2,1)S(1)}, u32[]{:S(2)}, u32[]{:S(2)}) collective-permute-start(bf16[27,8,256]{2,1,0:T(8,128)(2,1)S(1)} %bitcast.28), channel_id=1, source_target_pairs={{8,0},{265,1},{10,2},{267,3},{12,4},{269,5},{14,6},{271,7},{256,8}... | collective-permute-start | bytes 331784 | tf_op jit(solution)/shard_map/ppermute | solution.py:302
  35.8 26.5 %all-to-all-start.1 = ((bf16[8,256,256]{2,1,0:T(8,128)(2,1)}), bf16[8,256,256]{2,1,0:T(8,128)(2,1)S(1)}, u32[]{:S(2)}, u32[]{:S(2)}) async-start(bf16[8,256,256]{2,1,0:T(8,128)(2,1)} %broadcast_in_dim.7), calls=%async_computation.1 | async-start | bytes 2097152 | tf_op jit(solution)/shard_map/all_to_all | solution.py:307
  45.9 16.4 %copy-start.1 = (f32[512]{0:T(512)S(1)}, f32[512]{0:T(512)}, u32[]{:S(2)}) copy-start(f32[512]{0:T(512)} %param.7) | copy-start | bytes 6148
  66.3 19.1 %collective-permute-start.3 = (f32[8,128]{1,0:T(8,128)S(1)}, f32[8,128]{1,0:T(8,128)S(1)}, u32[]{:S(2)}, u32[]{:S(2)}) collective-permute-start(f32[8,128]{1,0:T(8,128)S(1)} %get-tuple-element.16), channel_id=1, source_target_pairs={{0,264},{2,266},{4,268},{6,270},{8,256},{10,258},{12,260},{14,262}... | collective-permute-start | bytes 12296 | tf_op jit(solution)/shard_map/ppermute | solution.py:332
  86.1 8.2 %all-to-all-start.2 = ((f32[4,8,128]{2,1,0:T(8,128)}), f32[4,8,128]{2,1,0:T(8,128)S(1)}, u32[]{:S(2)}, u32[]{:S(2)}) async-start(f32[4,8,128]{2,1,0:T(8,128)} %broadcast_in_dim.8), calls=%async_computation.2 | async-start | bytes 32768 | tf_op jit(solution)/shard_map/all_to_all | solution.py:335
  90.1 1.2 copy-start
Sparse Core Ops, SparseCore 0:
  22.5 60.7 all-gather.3

commit v6 on v5

--- a/solution.py
+++ b/solution.py
@@ -145,19 +145,11 @@
         precision=lax.Precision.HIGHEST,
         preferred_element_type=F32,
     )
-    gain_out_ref[...] = terms
-
-
-def low_kernel_body(
-    place_ref, grads_ref, edges_ref, weight_ref, out_ref, taps_ref
-):
-    to, at = iota((144, 112), 0), iota((144, 112), 1)
-    tap = 9 * (to // 48) + 3 * ((to >> 2) & 3) + (to >> 4) % 3
-    pick = jnp.where((at == 4 * tap + (to & 3)) & (((to >> 2) & 3) < 3), 1.0, 0.0).astype(BF16)
-    for n in range(8):
-        taps_ref[n] = jnp.dot(
-            pick, weight_ref[n, 0:112, :], preferred_element_type=F32
-        ).astype(BF16)
+    for n in range(4):
+        gain_out_ref[n] = terms
+
+
+def norm_body(place_ref, grads_ref, edges_ref, out_ref):
     c, z = place_ref[1], place_ref[2]
     source = iota((256, 256), 0)
     target = (
@@ -185,7 +177,18 @@
         scaled = mid * rms
         mean = jnp.mean(grad * scaled, axis=1, keepdims=True)
         halves.append((rms * (grad - scaled * mean)).astype(BF16))
-    grads = jnp.concatenate(halves, axis=0)
+    out_ref[...] = jnp.concatenate(halves, axis=0)
+
+
+def low_kernel_body(grads_ref, weight_ref, out_ref, taps_ref):
+    to, at = iota((144, 112), 0), iota((144, 112), 1)
+    tap = 9 * (to // 48) + 3 * ((to >> 2) & 3) + (to >> 4) % 3
+    pick = jnp.where((at == 4 * tap + (to & 3)) & (((to >> 2) & 3) < 3), 1.0, 0.0).astype(BF16)
+    for n in range(8):
+        taps_ref[n] = jnp.dot(
+            pick, weight_ref[n, 0:112, :], preferred_element_type=F32
+        ).astype(BF16)
+    grads = grads_ref[...]
     row = iota((512, 128), 0)
     frame = (row >> 2) & 15
     column = row & 3
@@ -319,7 +322,7 @@
         high_kernel_body,
         out_shape=(
             jax.ShapeDtypeStruct((256, 128), BF16),
-            jax.ShapeDtypeStruct((8, 128), F32),
+            jax.ShapeDtypeStruct((4, 8, 128), F32),
         ),
         in_specs=[scalars()] + [whole()] * 4,
         out_specs=(whole(), whole()),
@@ -333,18 +336,26 @@
     gathered = lax.all_gather(grads, group, axis=0)
     other, gathered = lax.optimization_barrier((other, gathered))
     clips = lax.all_to_all(
-        jnp.broadcast_to((gain_terms + other)[None], (4, 8, 128)), "y", split_axis=0, concat_axis=0, tiled=True
-    )
-
+        gain_terms + other, "y", split_axis=0, concat_axis=0, tiled=True
+    )
+
+    mid_grads = pl.pallas_call(
+        norm_body,
+        out_shape=jax.ShapeDtypeStruct((512, 512), BF16),
+        in_specs=[scalars(), whole(), whole()],
+        out_specs=whole(),
+        compiler_params=PARAMS,
+        name="norm",
+    )(place, gathered, edges)
     partial = pl.pallas_call(
         low_kernel_body,
         out_shape=jax.ShapeDtypeStruct((64, 4, 128), F32),
-        in_specs=[scalars(), whole(), whole(), whole()],
+        in_specs=[whole(), whole()],
         out_specs=whole(),
         scratch_shapes=[pltpu.VMEM((8, 144, 512), BF16)],
         compiler_params=PARAMS,
         name="low_conv",
-    )(place, gathered, edges, low_all)
+    )(mid_grads, low_all)
 
     outgoing = pl.pallas_call(
         close_body,

time: 125 us -> 125 us (level)
  no operation moved by 1% of the time
where the time goes in v6:
time: 125 us; the launch traced here: 124 us
  blocking collectives  52 us (42%)
  starting transfers between devices  38 us (30%)
  between operations  14.2 us (11%)
  Pallas kernels  8.48 us (7%)
  waiting for transfers between devices  5.89 us (5%)
  local copies, waits for them, and re-layouts  4.97 us (4%)
    all_to_all x1, blocking collectives, shards(): lax.all_to_all(outgoing, shard, split_axis=0, concat_axis=0, tiled=True)  21.5 us
    all_to_all x2, starting transfers between devices, spread(): lax.all_to_all(jnp.broadcast_to(block[None], (8, 256, 256)), group, split...  20.5 us
    all_gather x1, blocking collectives, shards(): high_all = lax.all_gather(high.reshape(432, 256), 'y', axis=0)  16.4 us
    all_gather x1, blocking collectives, shards(): gathered = lax.all_gather(grads, group, axis=0)  14.1 us
    ppermute x1, starting transfers between devices, shards(): far = lax.ppermute(high, ring, ring_pairs(FAR))  5.84 us
    ppermute x1, waiting for transfers between devices, shards(): far = lax.ppermute(high, ring, ring_pairs(FAR))  5.13 us
    ppermute x1, starting transfers between devices, shards(): other = lax.ppermute(gain_terms, ('zh', 'zl'), halves)  5.03 us
    all_to_all x1, starting transfers between devices, shards(): lax.all_to_all(gain_terms + other, 'y', split_axis=0, concat_axis=0, tile...  4.02 us
  transfers between devices with their start and end apart: 8, of which 2 were waited for; matrix products, arithmetic and copies ran while one was open for 2% of the time, Pallas kernels for 6%

profile of v6, /device:TPU:1, one launch (start us, length us, event | category | flops | bytes accessed | tf_op | source)
XLA Modules:
  0.0 124.2 jit_solution(6943149032682043532)
XLA Ops:
  7.2 0.9 copy.8
  8.1 1.0 broadcast_in_dim.4
  9.1 10.5 %all-to-all-start = ((bf16[8,256,256]{2,1,0:T(8,128)(2,1)}), bf16[8,256,256]{2,1,0:T(8,128)(2,1)S(1)}, u32[]{:S(2)}, u32[]{:S(2)}) async-start(bf16[8,256,256]{2,1,0:T(8,128)(2,1)} %broadcast_in_dim.4), calls=%async_computation | async-start | bytes 2097152 | tf_op jit(solution)/shard_map/all_to_all | solution.py:310
  19.7 0.7 pad.4
  20.3 1.9 %collective-permute-start = (bf16[256,256]{1,0:T(8,128)(2,1)S(1)}, bf16[256,256]{1,0:T(8,128)(2,1)S(1)}, u32[]{:S(2)}, u32[]{:S(2)}) collective-permute-start(bf16[256,256]{1,0:T(8,128)(2,1)S(1)} %bitcast.25), channel_id=1, source_target_pairs={{2,1},{4,3},{6,5},{8,7},{10,9},{12,11},{14,13},{16,15},{18,17},{20... | collective-permute-start | bytes 393224 | tf_op jit(solution)/shard_map/ppermute | solution.py:301
  22.3 0.7 collective-permute-start.1
  23.0 5.8 %collective-permute-start.2 = (bf16[27,8,256]{2,1,0:T(8,128)(2,1)S(1)}, bf16[27,8,256]{2,1,0:T(8,128)(2,1)S(1)}, u32[]{:S(2)}, u32[]{:S(2)}) collective-permute-start(bf16[27,8,256]{2,1,0:T(8,128)(2,1)S(1)} %bitcast.28), channel_id=1, source_target_pairs={{8,0},{265,1},{10,2},{267,3},{12,4},{269,5},{14,6},{271,7},{256,8}... | collective-permute-start | bytes 331784 | tf_op jit(solution)/shard_map/ppermute | solution.py:305
  28.9 5.1 %collective-permute-done.2 = bf16[27,8,256]{2,1,0:T(8,128)(2,1)S(1)} collective-permute-done((bf16[27,8,256]{2,1,0:T(8,128)(2,1)S(1)}, bf16[27,8,256]{2,1,0:T(8,128)(2,1)S(1)}, u32[]{:S(2)}, u32[]{:S(2)}) %collective-permute-start.2) | collective-permute-done | bytes 110624 | tf_op jit(solution)/shard_map/ppermute | solution.py:305
  34.0 0.7 all-to-all-done.parts_ref
  34.8 1.0 broadcast_in_dim.5
  35.8 10.1 %all-to-all-start.1 = ((bf16[8,256,256]{2,1,0:T(8,128)(2,1)}), bf16[8,256,256]{2,1,0:T(8,128)(2,1)S(1)}, u32[]{:S(2)}, u32[]{:S(2)}) async-start(bf16[8,256,256]{2,1,0:T(8,128)(2,1)} %broadcast_in_dim.5), calls=%async_computation.1 | async-start | bytes 2097152 | tf_op jit(solution)/shard_map/all_to_all | solution.py:310
  45.9 0.1 pad_add_fusion.place_ref
  46.0 16.4 %all_gather.15.weight_ref = bf16[4,432,256]{2,1,0:T(8,128)(2,1)S(1)} all-gather(bf16[1,432,256]{2,1,0:T(8,128)(2,1)S(1)} %bitcast.23), channel_id=1, replica_groups=mesh['zh'=2,'y'=4,'x'=4,'zl'=8,'c'=2] {'y'}, dimensions={0}, use_global_device_ids=true | all-gather | bytes 1105920 | tf_op jit(solution)/shard_map/all_gather | solution.py:320
  62.3 3.9 %high_conv.1 = (bf16[256,128]{1,0:T(8,128)(2,1)S(1)}, f32[4,8,128]{2,1,0:T(8,128)S(1)}) custom-call(s32[3]{0:T(128)S(1)} %pad_add_fusion.place_ref, bf16[8,256,256]{2,1,0:T(8,128)(2,1)S(1)} %all-to-all-done.parts_ref, bf16[8,256,256]{2,1,0:T(8,128)(2,1)S(1)} %all-to-all-done.1.edges_ref, bf16[4,432,256]{2,1,0:T(8,128)(2,1)S(1)} %all_gather.15.weight_ref, ...), custom_call_target="tpu_custom_call" | custom-call | tf_op jit(solution)/shard_map/high_conv/pallas_call | solution.py:321
  66.3 5.0 %collective-permute-start.3 = (f32[4,8,128]{2,1,0:T(8,128)S(1)}, f32[4,8,128]{2,1,0:T(8,128)S(1)}, u32[]{:S(2)}, u32[]{:S(2)}) collective-permute-start(f32[4,8,128]{2,1,0:T(8,128)S(1)} %get-tuple-element.16), channel_id=1, source_target_pairs={{0,264},{2,266},{4,268},{6,270},{8,256},{10,258},{12,260},{14,262}... | collective-permute-start | bytes 49160 | tf_op jit(solution)/shard_map/ppermute | solution.py:335
  71.3 14.1 %all-gather = bf16[2048,128]{1,0:T(8,128)(2,1)S(1)} all-gather(bf16[256,128]{1,0:T(8,128)(2,1)S(1)} %get-tuple-element.17), channel_id=2, replica_groups=mesh['zh'=2,'y'=4,'x'=4,'zl'=8,'c'=2] {'x','c'}, dimensions={0}, use_global_device_ids=true | all-gather | bytes 589824 | tf_op jit(solution)/shard_map/all_gather | solution.py:336
  85.4 0.6 add.5
  86.1 4.0 %all-to-all-start.2 = ((f32[4,8,128]{2,1,0:T(8,128)}), f32[4,8,128]{2,1,0:T(8,128)S(1)}, u32[]{:S(2)}, u32[]{:S(2)}) async-start(f32[4,8,128]{2,1,0:T(8,128)} %add.5), calls=%async_computation.2 | async-start | bytes 32768 | tf_op jit(solution)/shard_map/all_to_all | solution.py:338
  90.1 1.2 norm.1.grads_ref
  91.3 1.2 copy-done
  92.5 2.0 %low_conv.1.rows_ref = f32[64,4,128]{2,1,0:T(4,128)S(1)} custom-call(bf16[512,512]{1,0:T(8,128)(2,1)S(1)} %norm.1.grads_ref, bf16[8,128,512]{2,1,0:T(8,128)(2,1)S(1)} %bitcast.19), custom_call_target="tpu_custom_call" | custom-call | tf_op jit(solution)/shard_map/low_conv/pallas_call | solution.py:350
  94.5 0.1 close.1
  94.6 21.5 %all_to_all.20 = bf16[192,2,128]{2,1,0:T(2,128)(2,1)S(1)} all-to-all(bf16[192,2,128]{2,1,0:T(2,128)(2,1)S(1)} %bitcast.21), channel_id=1, replica_groups=mesh['zh'=2,'y'=4,'x'=4,'zl'=8,'c'=2] {'x','zl','c'}, dimensions={0} | all-to-all | bytes 196608 | tf_op jit(solution)/shard_map/all_to_all | solution.py:369
  116.1 1.3 %join.1 = (bf16[64,256]{1,0:T(8,128)(2,1)}, f32[4,128]{1,0:T(4,128)}) custom-call(bf16[64,3,2,128]{3,2,1,0:T(2,128)(2,1)S(1)} %bitcast.20), custom_call_target="tpu_custom_call" | custom-call | tf_op jit(solution)/shard_map/join/pallas_call | solution.py:372
  (23 shorter events, 0.2 us)
Async XLA Ops:
  9.1 10.5 %copy-start.2 = (bf16[4,27,512]{2,0,1:T(4,128)(2,1)S(1)}, bf16[4,27,512]{2,0,1:T(4,128)(2,1)}, u32[]{:S(2)}) copy-start(bf16[4,27,512]{2,0,1:T(4,128)(2,1)} %param.9) | copy-start | bytes 331780
  9.1 25.6 %all-to-all-start = ((bf16[8,256,256]{2,1,0:T(8,128)(2,1)}), bf16[8,256,256]{2,1,0:T(8,128)(2,1)S(1)}, u32[]{:S(2)}, u32[]{:S(2)}) async-start(bf16[8,256,256]{2,1,0:T(8,128)(2,1)} %broadcast_in_dim.4), calls=%async_computation | async-start | bytes 2097152 | tf_op jit(solution)/shard_map/all_to_all | solution.py:310
  19.6 71.7 %all-gather.4.cloned.1.call-start = ((), (), s32[]{:S(2)}) async-start(), calls=%async_computation.4 | async-start | bytes 1179648 | tf_op jit(solution)/shard_map/all_gather | solution.py:307
  19.6 2.6 %copy-start.4 = (bf16[8,27,256]{2,0,1:T(8,128)(2,1)S(1)}, bf16[8,27,256]{2,0,1:T(8,128)(2,1)}, u32[]{:S(2)}) copy-start(bf16[8,27,256]{2,0,1:T(8,128)(2,1)} %param.8) | copy-start | bytes 331780
  20.3 8.5 %copy-start.3 = (bf16[1,16,1,4,512]{4,3,2,1,0:T(4,128)(2,1)S(1)}, bf16[1,16,1,4,512]{4,3,2,1,0:T(4,128)(2,1)}, u32[]{:S(2)}) copy-start(bf16[1,16,1,4,512]{4,3,2,1,0:T(4,128)(2,1)} %param.6) | copy-start | bytes 196612
  20.3 13.7 %collective-permute-start = (bf16[256,256]{1,0:T(8,128)(2,1)S(1)}, bf16[256,256]{1,0:T(8,128)(2,1)S(1)}, u32[]{:S(2)}, u32[]{:S(2)}) collective-permute-start(bf16[256,256]{1,0:T(8,128)(2,1)S(1)} %bitcast.25), channel_id=1, source_target_pairs={{2,1},{4,3},{6,5},{8,7},{10,9},{12,11},{14,13},{16,15},{18,17},{20... | collective-permute-start | bytes 393224 | tf_op jit(solution)/shard_map/ppermute | solution.py:301
  22.3 6.6 %collective-permute-start.1 = (bf16[27,8,256]{2,1,0:T(8,128)(2,1)S(1)}, bf16[27,8,256]{2,1,0:T(8,128)(2,1)S(1)}, u32[]{:S(2)}, u32[]{:S(2)}) collective-permute-start(bf16[27,8,256]{2,1,0:T(8,128)(2,1)S(1)} %bitcast.27), channel_id=1, source_target_pairs={{0,0},{1,1},{2,2},{3,3},{4,4},{5,5},{6,6},{7,7},{8,8},{9,9},{10,10... | collective-permute-start | bytes 331784 | tf_op jit(solution)/shard_map/ppermute | solution.py:304
  23.0 11.0 %collective-permute-start.2 = (bf16[27,8,256]{2,1,0:T(8,128)(2,1)S(1)}, bf16[27,8,256]{2,1,0:T(8,128)(2,1)S(1)}, u32[]{:S(2)}, u32[]{:S(2)}) collective-permute-start(bf16[27,8,256]{2,1,0:T(8,128)(2,1)S(1)} %bitcast.28), channel_id=1, source_target_pairs={{8,0},{265,1},{10,2},{267,3},{12,4},{269,5},{14,6},{271,7},{256,8}... | collective-permute-start | bytes 331784 | tf_op jit(solution)/shard_map/ppermute | solution.py:305
  35.8 26.5 %all-to-all-start.1 = ((bf16[8,256,256]{2,1,0:T(8,128)(2,1)}), bf16[8,256,256]{2,1,0:T(8,128)(2,1)S(1)}, u32[]{:S(2)}, u32[]{:S(2)}) async-start(bf16[8,256,256]{2,1,0:T(8,128)(2,1)} %broadcast_in_dim.5), calls=%async_computation.1 | async-start | bytes 2097152 | tf_op jit(solution)/shard_map/all_to_all | solution.py:310
  45.9 16.4 %copy-start.1 = (f32[512]{0:T(512)S(1)}, f32[512]{0:T(512)}, u32[]{:S(2)}) copy-start(f32[512]{0:T(512)} %param.7) | copy-start | bytes 6148
  66.3 19.1 %collective-permute-start.3 = (f32[4,8,128]{2,1,0:T(8,128)S(1)}, f32[4,8,128]{2,1,0:T(8,128)S(1)}, u32[]{:S(2)}, u32[]{:S(2)}) collective-permute-start(f32[4,8,128]{2,1,0:T(8,128)S(1)} %get-tuple-element.16), channel_id=1, source_target_pairs={{0,264},{2,266},{4,268},{6,270},{8,256},{10,258},{12,260},{14,262}... | collective-permute-start | bytes 49160 | tf_op jit(solution)/shard_map/ppermute | solution.py:335
  86.1 8.4 %all-to-all-start.2 = ((f32[4,8,128]{2,1,0:T(8,128)}), f32[4,8,128]{2,1,0:T(8,128)S(1)}, u32[]{:S(2)}, u32[]{:S(2)}) async-start(f32[4,8,128]{2,1,0:T(8,128)} %add.5), calls=%async_computation.2 | async-start | bytes 32768 | tf_op jit(solution)/shard_map/all_to_all | solution.py:338
  91.3 1.2 copy-start
Sparse Core Ops, SparseCore 0:
  22.5 60.9 all-gather.3
